TPU v7x, 512 devices: a whole 4x4x16 slice. The times are simulated.
512 devices in a mesh: patch: 32 (over z, core), line: 16 (over x, y).
Axes of the slice: x: 4, y: 4, z: 16, core: 2. Of those that a mesh axis runs over, the one named last changes fastest.
Arguments:
- residual: float32 [128, 32, 100], P('patch', 'line'), may hold values from -2 to 2
- previous_adjoint: float32 [128, 32, 100], P('patch', 'line'), may hold values from -6 to 6
- lower_factor: float32 [128, 32, 100, 100], P('patch', 'line'), may hold values from -0.625 to 0.625
- pivot_inverse: float32 [128, 32, 100, 100], P('patch', 'line'), may hold values from -0.3 to 1.7, as said below
- upper_factor: float32 [128, 32, 100, 100], P('patch', 'line'), may hold values from -0.5 to 0.5
- face_couple: float32 [128, 32, 4, 100, 50], P('patch', 'line'), may hold values from -0.21875 to 0.21875
- face_restrict: float32 [4, 50, 100], replicated, may hold values from -0.625 to 0.625
- neighbours: int32 [128, 4], P('patch'), may hold values from 0 to 47
Outputs:
- adjoint: float32 [128, 32, 100], P('patch', 'line')
Inputs may be any that keep to these rules, and one draw needn't show every extreme that they name: `pivot_inverse`: each block is a diagonal between 0.6 and 1.4 plus a full part whose entries lie within 0.3 of zero.
All inputs are finite; a program needn't handle non-finite values.
Results may differ from a plain program's by a relative error of at most 0.00028.
Values sent between devices are 32-bit elements; how exact they have to be, the bound alone decides.
A program may use at most 64 MiB of HBM per device.

v0:
```python
import jax
import jax.numpy as jnp
from jax import lax
from jax.sharding import PartitionSpec as P

SWEEPS = 2


HIGH = lax.Precision.HIGHEST


def prefix(shard, axis, combine, identity, reverse):
    count, index = (lax.axis_size(axis), lax.axis_index(axis))
    everything = jax.tree.map(lambda part: lax.all_gather(part, axis), shard)
    start = jax.tree.map(
        lambda part, zero: jnp.broadcast_to(jnp.asarray(zero, part.dtype), part.shape),
        shard,
        identity,
    )

    def lap(k, before):
        at = count - 1 - k if reverse else k
        reached = at > index if reverse else at < index
        new = combine(before, jax.tree.map(lambda part: part[at], everything))
        return jax.tree.map(lambda a, b: jnp.where(reached, a, b), new, before)

    return lax.fori_loop(0, count, lap, start)


def with_halo(cells, sides, width):
    for axis, dim in sides:
        count = lax.axis_size(axis)
        head = lax.slice_in_dim(cells, 0, width, axis=dim)
        tail = lax.slice_in_dim(cells, cells.shape[dim] - width, cells.shape[dim], axis=dim)
        cells = jnp.concatenate(
            [
                lax.ppermute(tail, axis, [(i, (i + 1) % count) for i in range(count)]),
                cells,
                lax.ppermute(head, axis, [((i + 1) % count, i) for i in range(count)]),
            ],
            axis=dim,
        )
    return cells


def apply_block(block, vector):
    return jnp.einsum("nab,nb->na", block, vector, precision=HIGH)


def block_product(left, right):
    return jnp.einsum("nab,nbc->nac", left, right, precision=HIGH)


def forward_pass(lower_factor, rhs, start):
    previous = start
    values = []
    for index in range(rhs.shape[1]):
        previous = rhs[:, index] - apply_block(lower_factor[:, index], previous)
        values.append(previous)
    return jnp.stack(values, axis=1)


def backward_pass(pivot_inverse, upper_factor, ys, start):
    previous = start
    values = []
    for index in reversed(range(ys.shape[1])):
        inner = ys[:, index] - apply_block(upper_factor[:, index], previous)
        previous = apply_block(pivot_inverse[:, index], inner)
        values.append(previous)
    return jnp.stack(values[::-1], axis=1)


def segment_maps(pivot_inverse, upper_factor, lower_factor):
    count = lower_factor.shape[1]
    width = lower_factor.shape[2]
    identity = jnp.broadcast_to(
        jnp.eye(width, dtype=jnp.float32), (lower_factor.shape[0], width, width)
    )
    lower_map = identity
    for index in range(count):
        lower_map = block_product(-lower_factor[:, index], lower_map)
    upper_map = identity
    for index in reversed(range(count)):
        upper_map = block_product(
            -block_product(pivot_inverse[:, index], upper_factor[:, index]), upper_map
        )
    return (lower_map, upper_map, identity)


def compose(earlier, later):
    return (block_product(later[0], earlier[0]), apply_block(later[0], earlier[1]) + later[1])


def forward_entry(lower_map, tail, identity):
    _, entry = prefix((lower_map, tail), "line", compose, (identity, jnp.zeros_like(tail)), False)
    return entry


def backward_entry(upper_map, head, identity):
    _, entry = prefix((upper_map, head), "line", compose, (identity, jnp.zeros_like(head)), True)
    return entry


def coupling(field, face_restrict, face_couple, neighbours):
    own = jnp.einsum("fkb,nsb->nfsk", face_restrict, field, precision=HIGH)
    lines = own.shape[0]
    padded = with_halo(own, (("patch", 0),), lines)
    flat = padded.reshape(3 * lines * own.shape[1], own.shape[2], own.shape[3])
    picked = jnp.take(flat, neighbours, axis=0)
    return jnp.einsum("nsfbk,nfsk->nsb", face_couple, picked, precision=HIGH)


def per_device(
    residual,
    previous_adjoint,
    lower_factor,
    pivot_inverse,
    upper_factor,
    face_couple,
    face_restrict,
    neighbours,
):
    lower_map, upper_map, identity = segment_maps(pivot_inverse, upper_factor, lower_factor)
    zero_start = jnp.zeros((residual.shape[0], residual.shape[2]), jnp.float32)
    field = previous_adjoint
    for sweep in range(SWEEPS):
        rhs = residual - coupling(field, face_restrict, face_couple, neighbours)
        tail = forward_pass(lower_factor, rhs, zero_start)[:, -1]
        ys = forward_pass(lower_factor, rhs, forward_entry(lower_map, tail, identity))
        head = backward_pass(pivot_inverse, upper_factor, ys, zero_start)[:, 0]
        field = backward_pass(
            pivot_inverse, upper_factor, ys, backward_entry(upper_map, head, identity)
        )
    return field


def solution(mesh):
    placed = (
        P("patch", "line", None),
        P("patch", "line", None),
        P("patch", "line", None, None),
        P("patch", "line", None, None),
        P("patch", "line", None, None),
        P("patch", "line", None, None, None),
        P(),
        P("patch", None),
    )
    return jax.shard_map(
        per_device, mesh=mesh, in_specs=placed, out_specs=P("patch", "line", None), check_vma=False
    )
```

profile of v0, /device:TPU:6, one launch (start us, length us, event | category | flops | bytes accessed | tf_op | source)
XLA Modules:
  0.0 280.3 jit_solution(15354742759993403552)
XLA Ops:
  6.6 1.6 fusion.73
  11.4 8.9 %collective-permute-start.1 = (f32[4,4,2,50]{3,0,1,2:T(4,128)S(1)}, f32[4,4,2,50]{3,0,1,2:T(4,128)S(1)}, u32[]{:S(2)}, u32[]{:S(2)}) collective-permute-start(f32[4,4,2,50]{3,0,1,2:T(4,128)S(1)} %convolution_bitcast_fusion.2), channel_id=1, source_target_pairs={{16,0},{32,16},{48,32},{64,48},{80,64},{96,80},{112,96},{128,112},... | collective-permute-start | bytes 19208 | tf_op jit(solution)/shard_map/ppermute | solution.py:39
  20.3 2.1 fusion.74
  28.4 23.3 %all-gather.6 = f32[16,4,100]{2,1,0:T(4,128)S(1)} all-gather(f32[1,4,100]{2,1,0:T(4,128)S(1)} %subtract_bitcast_fusion.1), channel_id=3, replica_groups=mesh['patch'=32,'line'=16] {'line'}, dimensions={0}, use_global_device_ids=true | all-gather | bytes 27200 | tf_op jit(solution)/shard_map/all_gather | solution.py:14
  51.7 26.5 %all-gather.13.cloned.1.call-done = f32[64,100,100]{2,1,0:T(8,128)} async-done(((f32[4,100,100]{2,1,0:T(8,128)}), f32[64,100,100]{2,1,0:T(8,128)}) %all-gather.13.cloned.1.call-update) | async-done | bytes 2560016 | tf_op jit(solution)/shard_map/all_gather | solution.py:14
  78.2 22.7 %while.60 = (s32[]{:T(128)}, f32[4,100]{1,0:T(4,128)S(1)}, s32[]{:T(128)}, f32[16,4,100,100]{3,2,1,0:T(8,128)}, f32[16,4,100]{2,1,0:T(4,128)S(1)}, /*index=5*/s32[]{:T(128)}, s32[]{:T(128)}) while((s32[]{:T(128)}, f32[4,100]{1,0:T(4,128)S(1)}, s32[]{:T(128)}, f32[16,4,100,100]{3,2,1,0:T(8,128)}, f32[16,4,100]{2,1,0:T(4,128)S(1)}, ...), condition=%wide.region_1.3_spmd.clone, body=%wide.region_0.0_spmd.clone.sunk | while | flops 481604 | bytes 225906 | solution.py:27
  79.6 1.4 fusion.123
  81.0 1.4 fusion.123
  82.5 1.4 fusion.123
  83.9 1.4 fusion.123
  85.3 1.4 fusion.123
  86.7 1.4 fusion.123
  88.1 1.4 fusion.123
  89.6 1.4 fusion.123
  91.0 1.4 fusion.123
  92.4 1.4 fusion.123
  93.8 1.4 fusion.123
  95.2 1.4 fusion.123
  96.7 1.4 fusion.123
  98.1 1.4 fusion.123
  99.5 1.4 fusion.123
  103.1 21.6 %all-gather.7 = f32[16,4,100]{2,1,0:T(4,128)S(1)} all-gather(f32[1,4,100]{2,1,0:T(4,128)S(1)} %bitcast.383), channel_id=5, replica_groups=mesh['patch'=32,'line'=16] {'line'}, dimensions={0}, use_global_device_ids=true | all-gather | bytes 27200 | tf_op jit(solution)/shard_map/all_gather | solution.py:14
  124.8 19.6 %all-gather.15.cloned.1.call-done = f32[64,100,100]{2,1,0:T(8,128)} async-done(((f32[4,100,100]{2,1,0:T(8,128)}), f32[64,100,100]{2,1,0:T(8,128)}) %all-gather.15.cloned.1.call-update) | async-done | bytes 2560016 | tf_op jit(solution)/shard_map/all_gather | solution.py:14
  144.4 22.8 %while.61 = (s32[]{:T(128)}, f32[4,100]{1,0:T(4,128)S(1)}, s32[]{:T(128)}, f32[16,4,100,100]{3,2,1,0:T(8,128)}, f32[16,4,100]{2,1,0:T(4,128)S(1)}, /*index=5*/s32[]{:T(128)}, s32[]{:T(128)}, s32[]{:T(128)}, s32[]{:T(128)}) while((s32[]{:T(128)}, f32[4,100]{1,0:T(4,128)S(1)}, s32[]{:T(128)}, f32[16,4,100,100]{3,2,1,0:T(8,128)}, ...), condition=%wide.region_3.5_spmd.clone, body=%wide.region_2.4_spmd.clone.sunk | while | flops 481608 | bytes 225968 | solution.py:27
  150.1 1.4 fusion.127
  169.4 3.5 %collective-permute-start.3 = (f32[4,4,2,50]{3,0,1,2:T(4,128)S(1)}, f32[4,4,2,50]{3,0,1,2:T(4,128)S(1)}, u32[]{:S(2)}, u32[]{:S(2)}) collective-permute-start(f32[4,4,2,50]{3,0,1,2:T(4,128)S(1)} %convolution_bitcast_fusion.1), channel_id=1, source_target_pairs={{16,0},{32,16},{48,32},{64,48},{80,64},{96,80},{112,96},{128,112},... | collective-permute-start | bytes 19208 | tf_op jit(solution)/shard_map/ppermute | solution.py:39
  172.9 1.4 collective-permute-done.3
  174.4 2.9 %collective-permute-done.2 = f32[4,4,2,50]{3,0,1,2:T(4,128)S(1)} collective-permute-done((f32[4,4,2,50]{3,0,1,2:T(4,128)S(1)}, f32[4,4,2,50]{3,0,1,2:T(4,128)S(1)}, u32[]{:S(2)}, u32[]{:S(2)}) %collective-permute-start.2) | collective-permute-done | bytes 6432 | tf_op jit(solution)/shard_map/ppermute | solution.py:37
  179.5 21.3 %all-gather.8 = f32[16,4,100]{2,1,0:T(4,128)S(1)} all-gather(f32[1,4,100]{2,1,0:T(4,128)S(1)} %subtract_bitcast_fusion), channel_id=6, replica_groups=mesh['patch'=32,'line'=16] {'line'}, dimensions={0}, use_global_device_ids=true | all-gather | bytes 27200 | tf_op jit(solution)/shard_map/all_gather | solution.py:14
  200.7 22.7 %while.62 = (s32[]{:T(128)}, f32[4,100]{1,0:T(4,128)S(1)}, s32[]{:T(128)}, f32[16,4,100,100]{3,2,1,0:T(8,128)}, f32[16,4,100]{2,1,0:T(4,128)S(1)}, /*index=5*/s32[]{:T(128)}, s32[]{:T(128)}) while((s32[]{:T(128)}, f32[4,100]{1,0:T(4,128)S(1)}, s32[]{:T(128)}, f32[16,4,100,100]{3,2,1,0:T(8,128)}, f32[16,4,100]{2,1,0:T(4,128)S(1)}, ...), condition=%wide.region_5.7_spmd.clone, body=%wide.region_4.6_spmd.clone.sunk | while | flops 481604 | bytes 225906 | solution.py:27
  200.7 1.4 fusion.131
  202.1 1.4 fusion.131
  203.6 1.4 fusion.131
  205.0 1.4 fusion.131
  206.4 1.4 fusion.131
  207.8 1.4 fusion.131
  209.3 1.4 fusion.131
  210.7 1.4 fusion.131
  212.1 1.4 fusion.131
  213.5 1.4 fusion.131
  214.9 1.4 fusion.131
  216.4 1.4 fusion.131
  217.8 1.4 fusion.131
  219.2 1.4 fusion.131
  220.6 1.4 fusion.131
  222.0 1.4 fusion.131
  225.7 22.5 %all-gather.9 = f32[16,4,100]{2,1,0:T(4,128)S(1)} all-gather(f32[1,4,100]{2,1,0:T(4,128)S(1)} %bitcast.389), channel_id=7, replica_groups=mesh['patch'=32,'line'=16] {'line'}, dimensions={0}, use_global_device_ids=true | all-gather | bytes 27200 | tf_op jit(solution)/shard_map/all_gather | solution.py:14
  248.2 22.8 %while.63 = (s32[]{:T(128)}, f32[4,100]{1,0:T(4,128)S(1)}, s32[]{:T(128)}, f32[16,4,100,100]{3,2,1,0:T(8,128)}, f32[16,4,100]{2,1,0:T(4,128)S(1)}, /*index=5*/s32[]{:T(128)}, s32[]{:T(128)}, s32[]{:T(128)}, s32[]{:T(128)}) while((s32[]{:T(128)}, f32[4,100]{1,0:T(4,128)S(1)}, s32[]{:T(128)}, f32[16,4,100,100]{3,2,1,0:T(8,128)}, ...), condition=%wide.region_7.9_spmd.clone, body=%wide.region_6.8_spmd.clone.sunk | while | flops 481608 | bytes 225968 | solution.py:27
  248.2 1.4 fusion.135
  249.6 1.4 fusion.135
  251.0 1.4 fusion.135
  252.5 1.4 fusion.135
  253.9 1.4 fusion.135
  255.3 1.4 fusion.135
  256.7 1.4 fusion.135
  258.2 1.4 fusion.135
  259.6 1.4 fusion.135
  261.0 1.4 fusion.135
  262.5 1.4 fusion.135
  263.9 1.4 fusion.135
  265.3 1.4 fusion.135
  266.7 1.4 fusion.135
  268.2 1.4 fusion.135
  269.6 1.4 fusion.135
  (230 shorter events, 43.3 us)
Async XLA Ops:
  6.5 20.5 %copy-start = (f32[4,2,4,100,50]{3,2,4,1,0:T(4,128)S(1)}, f32[4,2,4,100,50]{3,2,4,1,0:T(4,128)}, u32[]{:S(2)}) copy-start(f32[4,2,4,100,50]{3,2,4,1,0:T(4,128)} %param.23) | copy-start | bytes 1920004
  6.5 71.7 %all-gather.13.cloned.1.call-start = ((), (), s32[]{:S(2)}) async-start(), calls=%async_computation | async-start | bytes 3620864 | tf_op jit(solution)/shard_map/all_gather | solution.py:14
  6.6 18.6 %copy-start.3 = (s32[4,4]{1,0:T(4,128)S(1)}, s32[4,4]{1,0:T(4,128)}, u32[]{:S(2)}) copy-start(s32[4,4]{1,0:T(4,128)} %param.25) | copy-start | bytes 196
  9.2 18.8 %copy-start.2 = (f32[4,2,100]{2,1,0:T(2,128)S(1)}, f32[4,2,100]{2,1,0:T(2,128)}, u32[]{:S(2)}) copy-start(f32[4,2,100]{2,1,0:T(2,128)} %param.18) | copy-start | bytes 9604
  10.0 134.3 %all-gather.15.cloned.1.call-start = ((), (), s32[]{:S(2)}) async-start(), calls=%async_computation.1 | async-start | bytes 3620864 | tf_op jit(solution)/shard_map/all_gather | solution.py:14
  11.4 14.8 %collective-permute-start.1 = (f32[4,4,2,50]{3,0,1,2:T(4,128)S(1)}, f32[4,4,2,50]{3,0,1,2:T(4,128)S(1)}, u32[]{:S(2)}, u32[]{:S(2)}) collective-permute-start(f32[4,4,2,50]{3,0,1,2:T(4,128)S(1)} %convolution_bitcast_fusion.2), channel_id=1, source_target_pairs={{16,0},{32,16},{48,32},{64,48},{80,64},{96,80},{112,96},{128,112},... | collective-permute-start | bytes 19208 | tf_op jit(solution)/shard_map/ppermute | solution.py:39
  20.3 5.9 %collective-permute-start = (f32[4,4,2,50]{3,0,1,2:T(4,128)S(1)}, f32[4,4,2,50]{3,0,1,2:T(4,128)S(1)}, u32[]{:S(2)}, u32[]{:S(2)}) collective-permute-start(f32[4,4,2,50]{3,0,1,2:T(4,128)S(1)} %convolution_bitcast_fusion.2), channel_id=1, source_target_pairs={{0,16},{16,32},{32,48},{48,64},{64,80},{80,96},{96,112},{112,128},... | collective-permute-start | bytes 19208 | tf_op jit(solution)/shard_map/ppermute | solution.py:37
  25.2 143.8 %copy-start.1 = (f32[4,50,100]{2,0,1:T(4,128)S(1)}, f32[4,50,100]{2,0,1:T(4,128)}, u32[]{:S(2)}) copy-start(f32[4,50,100]{2,0,1:T(4,128)} %param.24) | copy-start | bytes 240004
  169.4 5.0 %collective-permute-start.3 = (f32[4,4,2,50]{3,0,1,2:T(4,128)S(1)}, f32[4,4,2,50]{3,0,1,2:T(4,128)S(1)}, u32[]{:S(2)}, u32[]{:S(2)}) collective-permute-start(f32[4,4,2,50]{3,0,1,2:T(4,128)S(1)} %convolution_bitcast_fusion.1), channel_id=1, source_target_pairs={{16,0},{32,16},{48,32},{64,48},{80,64},{96,80},{112,96},{128,112},... | collective-permute-start | bytes 19208 | tf_op jit(solution)/shard_map/ppermute | solution.py:39
  172.9 4.4 %collective-permute-start.2 = (f32[4,4,2,50]{3,0,1,2:T(4,128)S(1)}, f32[4,4,2,50]{3,0,1,2:T(4,128)S(1)}, u32[]{:S(2)}, u32[]{:S(2)}) collective-permute-start(f32[4,4,2,50]{3,0,1,2:T(4,128)S(1)} %convolution_bitcast_fusion.1), channel_id=1, source_target_pairs={{0,16},{16,32},{32,48},{48,64},{64,80},{80,96},{96,112},{112,128},... | collective-permute-start | bytes 19208 | tf_op jit(solution)/shard_map/ppermute | solution.py:37
Sparse Core Ops, SparseCore 0:
  10.4 67.7 all-gather.12
  81.2 63.0 all-gather.14
where the time goes:
time: 282 us; the launch traced here: 280 us
  matrix products  105 us (37%)
  blocking collectives  88.6 us (31%)
  waiting for transfers between devices  50.6 us (18%)
  between operations  13.7 us (5%)
  starting transfers between devices  12.5 us (4%)
  local copies, waits for them, and re-layouts  5.88 us (2%)
    dot_general x86, matrix products, apply_block(): return jnp.einsum('nab,nb->na', block, vector, precision=HIGH)  97.5 us
    all_gather x4, blocking collectives, prefix(): everything = jax.tree.map(lambda part: lax.all_gather(part, axis), shard)  88.6 us
    all_gather x2, waiting for transfers between devices, prefix(): everything = jax.tree.map(lambda part: lax.all_gather(part, axis), shard)  46.2 us
    ppermute x2, starting transfers between devices, with_halo(): lax.ppermute(head, axis, [((i + 1) % count, i) for i in range(count)])  12.4 us
  transfers between devices with their start and end apart: 6, of which 4 were waited for; matrix products, arithmetic and copies ran while one was open for 12% of the time, Pallas kernels for 0%

commit v1 on v0

v1 whole, which is shorter than its diff:
```python
import jax
import jax.numpy as jnp
from jax import lax
from jax.experimental import pallas as pl
from jax.experimental.pallas import tpu as pltpu
from jax.sharding import PartitionSpec as P

F32 = jnp.float32
BF16 = jnp.bfloat16
MESH = pl.DeviceIdType.MESH
B = 100
Q = 200
NP = 32
NN = (((1,), (0,)), ((), ()))
NT = (((1,), (1,)), ((), ()))


def split(a):
    high = a.astype(BF16)
    return high, (a - high.astype(F32)).astype(BF16)


def dot3(a, b, dims):
    ah, al = split(a)
    bh, bl = split(b)

    def mm(u, v):
        return lax.dot_general(u, v, dims, preferred_element_type=F32)

    return mm(ah, bh) + (mm(ah, bl) + mm(al, bh))


def kernel(
    nb, res, prev, low, piv, upp, fc, rst, out,
    rl, rd, ru, rf, fown, hb, rhs_out, rhs_in, eb, zxb, zs, hb2, th, fx, f8, lhs, ob,
    s_loc, s_raw, r_raw, s_h0, r_h0, s_a, r_a, s_x, r_x, s_h1, r_h1, s_t, r_t, s_o, r_o,
):
    p = lax.axis_index("patch")
    line = lax.axis_index("line")
    x, y = line // 4, line % 4

    def y_peer(d):
        return (p, x * 4 + (y + d) % 4)

    def x_peer(d):
        return (p, ((x + d) % 4) * 4 + y)

    def remote(src, dst, send, recv, device):
        return pltpu.make_async_remote_copy(
            src_ref=src, dst_ref=dst, send_sem=send, recv_sem=recv,
            device_id=device, device_id_type=MESH,
        )

    raws = ((low, rl), (piv, rd), (upp, ru), (fc, rf))
    local = [pltpu.make_async_copy(fc, fown, s_loc.at[4])]
    for k, (src, dst) in enumerate(raws):
        local.append(pltpu.make_async_copy(src.at[y], dst.at[y], s_loc.at[k]))
    for copy in local:
        copy.start()

    around = [
        (dp, dy) for dp in (-1, 0, 1) for dy in range(4) if (dp, dy) != (0, 0)
    ]

    def around_peer(dp, dy):
        return ((p + dp + NP) % NP, x * 4 + (y + dy) % 4)

    barrier = pltpu.get_barrier_semaphore()
    for dp, dy in around:
        pl.semaphore_signal(
            barrier, inc=1, device_id=around_peer(dp, dy), device_id_type=MESH
        )
    for d in (1, 2, 3):
        pl.semaphore_signal(barrier, inc=1, device_id=x_peer(d), device_id_type=MESH)

    halo = dot3(prev[...], rst[...], NT)
    for n in range(4):
        hb[4 + n, :, :Q] = halo[2 * n : 2 * n + 2]
    pl.semaphore_wait(barrier, 14)

    sends = []
    halos = []
    for i, dp in enumerate((1, -1)):
        copy = remote(
            hb.at[pl.ds(4, 4)], hb.at[pl.ds((1 - dp) * 4, 4)], s_h0.at[i], r_h0.at[i],
            ((p + dp + NP) % NP, line),
        )
        copy.start()
        halos.append(copy)
    sends += halos
    raw = {}
    for k, (src, dst) in enumerate(raws):
        for d in (1, 3, 2):
            copy = remote(
                src.at[(y + d) % 4], dst.at[y], s_raw.at[k, d - 1], r_raw.at[k, d - 1],
                y_peer(d),
            )
            copy.start()
            raw[k, d] = copy
            sends.append(copy)

    lane = lax.broadcasted_iota(jnp.int32, (8, Q), 1) % 4

    def pick(block, source, f):
        total = jnp.zeros(block.shape, F32)
        for g in range(4):
            moved = block if g == f else pltpu.roll(block, (f - g) % 256, axis=1)
            total = jnp.where(source == g, moved, total)
        return jnp.where(lane[: block.shape[0]] == f, total[:, :Q], 0.0)

    for copy in halos:
        copy.wait_recv()
    for n in range(4):
        picked = jnp.zeros((2, Q), F32)
        for f in range(4):
            entry = nb[n, f]
            picked = picked + pick(hb[entry // 4], entry % 4, f)
        lhs[2 * n : 2 * n + 2, :Q] = picked
    local[0].wait()
    whole = lhs[:, :Q]
    for n in range(4):
        for e in range(2):
            row = 2 * n + e
            got = dot3(whole, fown[n, e], NN)
            rhs_out[n, e : e + 1, :B] = res[row : row + 1, :] - got[row : row + 1, :]
        rhs_out[n, 2:4, :B] = res[2 * n : 2 * n + 2, :]
    rhs_in[y] = rhs_out[y]
    there = []
    for d in (1, 3, 2):
        copy = remote(
            rhs_out.at[(y + d) % 4], rhs_in.at[y], s_a.at[d - 1], r_a.at[d - 1], y_peer(d)
        )
        copy.start()
        there.append(copy)
    sends += there

    for copy in local[1:4]:
        copy.wait()
    for k in range(3):
        for d in (1, 3, 2):
            raw[k, d].wait_recv()

    def block(ref, l):
        return ref[l // 2, pl.ds(l % 2, B, stride=2), :]

    for l in range(8):
        eb[l, :B, :B] = dot3(block(rd, l), block(ru, l), NN)
    for copy in there:
        copy.wait_recv()

    rows = lax.broadcasted_iota(jnp.int32, (104, B), 0)
    columns = lax.broadcasted_iota(jnp.int32, (104, B), 1)
    unit = jnp.where(rows == columns, 1.0, 0.0).astype(F32)
    eye = rows[:B] == columns[:B]

    def rhs_row(l):
        return rhs_in[l // 2, l % 2 : l % 2 + 1, :B]

    zy = unit
    for l in range(8):
        zy = jnp.where(rows == B, rhs_row(l), 0.0) - dot3(zy, block(rl, l), NT)
        zxb[l, :104, :B] = dot3(zy, block(rd, l), NT)
    zs[x, :104, :B] = zy
    after = jnp.concatenate([jnp.zeros((104, B), F32), unit], axis=0)
    for l in range(7, -1, -1):
        moved = dot3(after, eb[l, :B, :B], NT)
        after = jnp.concatenate([zxb[l, :104, :B] - moved[:104], -moved[104:]], axis=0)
        zxb[l, :, :B] = after
    zs[x, 104:, :B] = after
    there = []
    for d in (1, 3, 2):
        copy = remote(zs.at[x], zs.at[x], s_x.at[d - 1], r_x.at[d - 1], x_peer(d))
        copy.start()
        there.append(copy)
    sends += there

    def column(row):
        return jnp.sum(jnp.where(eye, row, 0.0), axis=1, keepdims=True)

    def times(row, matrix):
        return jnp.sum(matrix * column(row), axis=0, keepdims=True)

    def apply(matrix, row):
        got = jnp.sum(matrix * row, axis=1, keepdims=True)
        return jnp.sum(jnp.where(eye, got, 0.0), axis=0, keepdims=True)

    def entries(tail, head):
        y2 = tail[1] + times(tail[0], zs[1, :B, :B])
        y3 = tail[2] + times(y2, zs[2, :B, :B])
        h3 = head[3] + times(y3, zs[3, 104:204, :B])
        h2 = head[2] + times(y2, zs[2, 104:204, :B]) + times(h3, zs[2, 208:308, :B])
        h1 = head[1] + times(tail[0], zs[1, 104:204, :B]) + times(h2, zs[1, 208:308, :B])
        zero = jnp.zeros((1, B), F32)

        def mine(values):
            total = values[0]
            for at in range(1, 4):
                total = jnp.where(x == at, values[at], total)
            return total

        return mine((zero, tail[0], y2, y3)), mine((h1, h2, h3, zero))

    def corrected(base, y_in, x_in):
        y_col, x_col = column(y_in), column(x_in)
        values = []
        for l in range(8):
            more = zxb[l, :B, :B] * y_col + zxb[l, 104:204, :B] * x_col
            values.append(base[l] + jnp.sum(more, axis=0, keepdims=True))
        return values

    for copy in there:
        copy.wait_recv()
    y_in, x_in = entries(
        [zs[at, B : B + 1, :B] for at in range(4)],
        [zs[at, 204:205, :B] for at in range(4)],
    )
    field = corrected([zxb[l, B : B + 1, :B] for l in range(8)], y_in, x_in)
    for l in range(8):
        f8[l : l + 1, :B] = field[l]

    hb2[4 + y, :, :Q] = dot3(f8[:, :B], rst[...], NT)
    there = []
    for i, (dp, dy) in enumerate(around):
        copy = remote(
            hb2.at[4 + y], hb2.at[(1 - dp) * 4 + y], s_h1.at[i], r_h1.at[i], around_peer(dp, dy)
        )
        copy.start()
        there.append(copy)
    sends += there
    local[4].wait()
    for d in (1, 3, 2):
        raw[3, d].wait_recv()
    for copy in there:
        copy.wait_recv()
    picked = jnp.zeros((8, Q), F32)
    for f in range(4):
        entry = nb[y, f]
        picked = picked + pick(hb2[entry // 4], entry % 4, f)
    ys = []
    for l in range(8):
        got = dot3(picked, rf[l // 2, l % 2], NN)
        value = res_owner(l, rhs_in) - got[l : l + 1, :]
        if l:
            value = value - apply(block(rl, l), ys[-1])
        ys.append(value)
    base = [None] * 8
    for l in range(7, -1, -1):
        base[l] = apply(block(rd, l), ys[l])
        if l < 7:
            base[l] = base[l] - apply(eb[l, :B, :B], base[l + 1])
    th[x, 0:1, :B] = ys[7]
    th[x, 1:2, :B] = base[0]
    there = []
    for d in (1, 3, 2):
        copy = remote(th.at[x], th.at[x], s_t.at[d - 1], r_t.at[d - 1], x_peer(d))
        copy.start()
        there.append(copy)
    sends += there
    for copy in there:
        copy.wait_recv()
    y_in, x_in = entries(
        [th[at, 0:1, :B] for at in range(4)], [th[at, 1:2, :B] for at in range(4)]
    )
    field = corrected(base, y_in, x_in)
    for l in range(8):
        fx[l // 2, l % 2 : l % 2 + 1, :B] = field[l]
    ob[y] = fx[y]
    there = []
    for d in (1, 3, 2):
        copy = remote(fx.at[(y + d) % 4], ob.at[y], s_o.at[d - 1], r_o.at[d - 1], y_peer(d))
        copy.start()
        there.append(copy)
    sends += there
    for copy in there:
        copy.wait_recv()
    for n in range(4):
        out[2 * n : 2 * n + 2, :] = ob[n, :, :B]
    for copy in sends:
        copy.wait_send()


def res_owner(l, ref):
    return ref[l // 2, 2 + l % 2 : 3 + l % 2, :B]


def per_device(residual, previous, lower, pivot, upper, couple, restrict, neighbours):
    def factor(a):
        return jnp.transpose(a, (0, 2, 1, 3)).reshape(4, 2 * B, B)

    vmem = pl.BlockSpec(memory_space=pltpu.VMEM)
    anywhere = pl.BlockSpec(memory_space=pl.ANY)
    dma = pltpu.SemaphoreType.DMA
    result = pl.pallas_call(
        kernel,
        out_shape=jax.ShapeDtypeStruct((8, B), F32),
        in_specs=[pl.BlockSpec(memory_space=pltpu.SMEM), vmem, vmem]
        + [anywhere] * 4
        + [vmem],
        out_specs=vmem,
        scratch_shapes=[
            pltpu.VMEM((4, 2 * B, B), F32),
            pltpu.VMEM((4, 2 * B, B), F32),
            pltpu.VMEM((4, 2 * B, B), F32),
            pltpu.VMEM((4, 2, Q, B), F32),
            pltpu.VMEM((4, 2, Q, B), F32),
            pltpu.VMEM((12, 2, 256), F32),
            pltpu.VMEM((4, 4, 128), F32),
            pltpu.VMEM((4, 4, 128), F32),
            pltpu.VMEM((8, 104, 128), F32),
            pltpu.VMEM((8, 208, 128), F32),
            pltpu.VMEM((4, 312, 128), F32),
            pltpu.VMEM((12, 8, 256), F32),
            pltpu.VMEM((4, 8, 128), F32),
            pltpu.VMEM((4, 2, 128), F32),
            pltpu.VMEM((8, 128), F32),
            pltpu.VMEM((8, 256), F32),
            pltpu.VMEM((4, 2, 128), F32),
            dma((5,)),
            dma((4, 3)),
            dma((4, 3)),
            dma((2,)),
            dma((2,)),
            dma((3,)),
            dma((3,)),
            dma((3,)),
            dma((3,)),
            dma((11,)),
            dma((11,)),
            dma((3,)),
            dma((3,)),
            dma((3,)),
            dma((3,)),
        ],
        compiler_params=pltpu.CompilerParams(
            collective_id=0, has_side_effects=True, vmem_limit_bytes=40 << 20
        ),
    )(
        neighbours,
        residual.reshape(8, B),
        previous.reshape(8, B),
        factor(lower),
        factor(pivot),
        factor(upper),
        jnp.transpose(couple, (0, 1, 4, 2, 3)).reshape(4, 2, Q, B),
        jnp.transpose(restrict, (1, 0, 2)).reshape(Q, B),
    )
    return result.reshape(4, 2, B)


def solution(mesh):
    placed = (
        P("patch", "line", None),
        P("patch", "line", None),
        P("patch", "line", None, None),
        P("patch", "line", None, None),
        P("patch", "line", None, None),
        P("patch", "line", None, None, None),
        P(),
        P("patch", None),
    )
    return jax.shard_map(
        per_device, mesh=mesh, in_specs=placed, out_specs=P("patch", "line", None), check_vma=False
    )
```

time: 282 us -> 70.9 us (0.25)
  matrix products: 105 us -> 0 us
  blocking collectives: 88.6 us -> 0 us
  Pallas kernels: 0 us -> 64.2 us
  waiting for transfers between devices: 50.6 us -> 0 us
  between operations: 13.7 us -> 0.02 us
  starting transfers between devices: 12.5 us -> 0 us
    dot_general x96 -> x0, matrix products: 105 us -> none  [the longest x86 97.5 us: apply_block(): return jnp.einsum('nab,nb->na', block, vector, precision=HIGH)]
    all_gather x4 -> x0, blocking collectives: 88.6 us -> none  [prefix(): everything = jax.tree.map(lambda part: lax.all_gather(part, axis), shard)]
    pallas_call x0 -> x1, Pallas kernels: none -> 64.2 us  [per_device(): pl.pallas_call(kernel, out_shape=jax.ShapeDtypeStruct((8, B), F32), in_sp...]
    all_gather x2 -> x0, waiting for transfers between devices: 46.2 us -> none  [prefix(): everything = jax.tree.map(lambda part: lax.all_gather(part, axis), shard)]
    ppermute x4 -> x0, starting transfers between devices: 12.4 us -> none  [the longest x2 12.4 us: with_halo(): lax.ppermute(head, axis, [((i + 1) % count, i) for i in range(count)])]
    unnamed x8 -> x17, local copies, waits for them, and re-layouts: 0.02 us -> 6.35 us
    ppermute x4 -> x0, waiting for transfers between devices: 4.37 us -> none  [the longest x2 2.93 us: with_halo(): lax.ppermute(tail, axis, [(i, (i + 1) % count) for i in range(count)])]
    slice x2 -> x0, local copies, waits for them, and re-layouts: 3.67 us -> none  [the longest x1 2.11 us: backward_pass(): previous = apply_block(pivot_inverse[:, index], inner)]
  transfers between devices with their start and end apart: 6 -> 0, of which waited for: 4 -> 0; matrix products, arithmetic and copies ran while one was open for 12% -> 0% of each run, Pallas kernels for 0% -> 0%
where the time goes in v1:
time: 70.9 us; the launch traced here: 70.5 us
  Pallas kernels  64.2 us (91%)
  local copies, waits for them, and re-layouts  6.35 us (9%)
    pallas_call x1, Pallas kernels, per_device(): pl.pallas_call(kernel, out_shape=jax.ShapeDtypeStruct((8, B), F32), in_sp...  64.2 us
    unnamed x17, local copies, waits for them, and re-layouts  6.35 us

profile of v1, /device:TPU:6, one launch (start us, length us, event | category | flops | bytes accessed | tf_op | source)
XLA Modules:
  0.0 70.5 jit_solution(9361146002298536493)
XLA Ops:
  0.0 0.0 copy-start.7
  0.0 0.0 copy-start.6
  0.0 0.0 copy-start.5
  0.0 0.7 copy-done.7
  0.7 0.0 copy-done.6
  0.7 0.0 copy-done.5
  0.7 0.0 copy-start
  0.7 1.1 %copy-done = f32[4,2,4,100,50]{3,2,4,1,0:T(4,128)S(1)} copy-done((f32[4,2,4,100,50]{3,2,4,1,0:T(4,128)S(1)}, f32[4,2,4,100,50]{3,2,4,1,0:T(4,128)}, u32[]{:S(2)}) %copy-start) | copy-done | bytes 640024
  1.9 0.0 copy-start.1
  1.9 1.0 %copy-done.1 = f32[4,2,100,100]{3,1,2,0:T(2,128)S(1)} copy-done((f32[4,2,100,100]{3,1,2,0:T(2,128)S(1)}, f32[4,2,100,100]{3,1,2,0:T(2,128)}, u32[]{:S(2)}) %copy-start.1) | copy-done | bytes 320024
  2.9 0.0 copy-start.2
  2.9 1.0 %copy-done.2 = f32[4,2,100,100]{3,1,2,0:T(2,128)S(1)} copy-done((f32[4,2,100,100]{3,1,2,0:T(2,128)S(1)}, f32[4,2,100,100]{3,1,2,0:T(2,128)}, u32[]{:S(2)}) %copy-start.2) | copy-done | bytes 320024
  3.9 0.0 copy-start.3
  3.9 1.0 %copy-done.3 = f32[4,2,100,100]{3,1,2,0:T(2,128)S(1)} copy-done((f32[4,2,100,100]{3,1,2,0:T(2,128)S(1)}, f32[4,2,100,100]{3,1,2,0:T(2,128)}, u32[]{:S(2)}) %copy-start.3) | copy-done | bytes 320024
  4.9 0.0 copy-start.4
  4.9 0.9 %copy-done.4 = f32[4,50,100]{2,0,1:T(4,128)S(1)} copy-done((f32[4,50,100]{2,0,1:T(4,128)S(1)}, f32[4,50,100]{2,0,1:T(4,128)}, u32[]{:S(2)}) %copy-start.4) | copy-done | bytes 80024
  5.8 64.2 %shard_map.82 = f32[8,100]{1,0:T(8,128)S(1)} custom-call(s32[4,4]{1,0:T(4,128)S(1)} %copy-done.7, f32[8,100]{1,0:T(8,128)S(1)} %bitcast.24, f32[8,100]{1,0:T(8,128)S(1)} %bitcast.25, f32[4,200,100]{2,1,0:T(8,128)S(1)} %bitcast.19, f32[4,200,100]{2,1,0:T(8,128)S(1)} %bitcast.20, f32[4,200,100]{2,1,0:T(8,128)S(1)} %bitcast.21, ...), custom_call_target="tpu_custom_call" | custom-call | tf_op jit(solution)/shard_map/pallas_call | solution.py:293
  69.9 0.6 copy.10
Async XLA Ops:
  0.0 0.7 copy-start.7
  0.0 0.7 copy-start.6
  0.0 0.7 %copy-start.5 = (f32[4,2,100]{2,1,0:T(2,128)S(1)}, f32[4,2,100]{2,1,0:T(2,128)}, u32[]{:S(2)}) copy-start(f32[4,2,100]{2,1,0:T(2,128)} %param.8) | copy-start | bytes 9604
  0.7 1.1 %copy-start = (f32[4,2,4,100,50]{3,2,4,1,0:T(4,128)S(1)}, f32[4,2,4,100,50]{3,2,4,1,0:T(4,128)}, u32[]{:S(2)}) copy-start(f32[4,2,4,100,50]{3,2,4,1,0:T(4,128)} %param.13) | copy-start | bytes 1920004
  1.9 1.0 %copy-start.1 = (f32[4,2,100,100]{3,1,2,0:T(2,128)S(1)}, f32[4,2,100,100]{3,1,2,0:T(2,128)}, u32[]{:S(2)}) copy-start(f32[4,2,100,100]{3,1,2,0:T(2,128)} %param.10) | copy-start | bytes 960004
  2.9 1.0 %copy-start.2 = (f32[4,2,100,100]{3,1,2,0:T(2,128)S(1)}, f32[4,2,100,100]{3,1,2,0:T(2,128)}, u32[]{:S(2)}) copy-start(f32[4,2,100,100]{3,1,2,0:T(2,128)} %param.11) | copy-start | bytes 960004
  3.9 1.0 %copy-start.3 = (f32[4,2,100,100]{3,1,2,0:T(2,128)S(1)}, f32[4,2,100,100]{3,1,2,0:T(2,128)}, u32[]{:S(2)}) copy-start(f32[4,2,100,100]{3,1,2,0:T(2,128)} %param.12) | copy-start | bytes 960004
  4.9 0.9 %copy-start.4 = (f32[4,50,100]{2,0,1:T(4,128)S(1)}, f32[4,50,100]{2,0,1:T(4,128)}, u32[]{:S(2)}) copy-start(f32[4,50,100]{2,0,1:T(4,128)} %param.14) | copy-start | bytes 240004

commit v2 on v0

v2 whole, which is shorter than its diff:
```python
import jax
import jax.numpy as jnp
from jax import lax
from jax.experimental import pallas as pl
from jax.experimental.pallas import tpu as pltpu
from jax.sharding import PartitionSpec as P

F32 = jnp.float32
BF16 = jnp.bfloat16
MESH = pl.DeviceIdType.MESH
B = 100
Q = 200
NP = 32
NN = (((1,), (0,)), ((), ()))
NT = (((1,), (1,)), ((), ()))
ORDER = (1, 3, 2)


def split(a):
    high = a.astype(BF16)
    return high, (a - high.astype(F32)).astype(BF16)


def dot3(a, b, dims=NN):
    ah, al = split(a)
    bh, bl = split(b)

    def mm(u, v):
        return lax.dot_general(u, v, dims, preferred_element_type=F32)

    return mm(ah, bh) + (mm(ah, bl) + mm(al, bh))


def kernel(
    nb_any, res_any, prev_any, rst_any, low, piv, upp, fc, out,
    nb, res, prev, rst, lo, di, up, fo,
    eb, wb, seg_out, seg_in, quarter, part, hb_first, hb_second, lhs, f8,
    a_out, a_in, th, en_out, en_in,
    s_loc, s_m, r_m, s_q, r_q, s_h, r_h, s_a, r_a, s_x, r_x, s_e, r_e,
):
    p = lax.axis_index("patch")
    line = lax.axis_index("line")
    x, y = line // 4, line % 4

    def y_peer(d):
        return (p, x * 4 + (y + d) % 4)

    def x_peer(d):
        return (p, ((x + d) % 4) * 4 + y)

    def z_peer(d):
        return ((p + d + NP) % NP, line)

    def remote(src, dst, send, recv, device):
        return pltpu.make_async_remote_copy(
            src_ref=src, dst_ref=dst, send_sem=send, recv_sem=recv,
            device_id=device, device_id_type=MESH,
        )

    barrier = pltpu.get_barrier_semaphore()
    for d in (1, 2, 3):
        pl.semaphore_signal(barrier, inc=1, device_id=y_peer(d), device_id_type=MESH)
        pl.semaphore_signal(barrier, inc=1, device_id=x_peer(d), device_id_type=MESH)
    for d in (1, -1):
        pl.semaphore_signal(barrier, inc=1, device_id=z_peer(d), device_id_type=MESH)
    pairs = (
        (low, lo), (prev_any, prev), (rst_any, rst), (piv, di), (upp, up),
        (nb_any, nb), (res_any, res), (fc, fo),
    )
    local = [
        pltpu.make_async_copy(src, dst, s_loc.at[k]) for k, (src, dst) in enumerate(pairs)
    ]
    for copy in local:
        copy.start()

    hb = (hb_first, hb_second)
    sends = []
    eye = lax.broadcasted_iota(jnp.int32, (B, B), 0) == lax.broadcasted_iota(
        jnp.int32, (B, B), 1
    )

    def to_row(column):
        return jnp.sum(jnp.where(eye, column, 0.0), axis=0, keepdims=True)

    def apply(matrix, row):
        return to_row(jnp.sum(matrix * row, axis=1, keepdims=True))

    def apply2(one, u, two, v):
        return to_row(jnp.sum(one * u + two * v, axis=1, keepdims=True))

    def element(ref, n, l):
        return ref[n, pl.ds(l, B, stride=2), :]

    def seg(k, j):
        return seg_in[k, j, :B, :B]

    def own(k, n):
        return seg_out[k, n, :B, :B]

    def send_halo(sweep, field):
        halo = dot3(field, rst[...], NT)
        for n in range(4):
            hb[sweep][4 + n, :, :Q] = halo[2 * n : 2 * n + 2]
        if sweep == 0:
            pl.semaphore_wait(barrier, 8)
        copies = []
        for i, dp in enumerate((1, -1)):
            copy = remote(
                hb[sweep].at[pl.ds(4, 4)], hb[sweep].at[pl.ds((1 - dp) * 4, 4)],
                s_h.at[sweep, i], r_h.at[sweep, i], z_peer(dp),
            )
            copy.start()
            copies.append(copy)
        sends.extend(copies)
        return copies

    def send_maps(k):
        copies = []
        for d in ORDER:
            copy = remote(
                seg_out.at[k, (y + d) % 4], seg_in.at[k, y],
                s_m.at[k, d - 1], r_m.at[k, d - 1], y_peer(d),
            )
            copy.start()
            copies.append(copy)
        sends.extend(copies)
        seg_in[k, y] = seg_out[k, y]
        return copies

    def send_quarter(k, value):
        quarter[x, k, :B, :B] = value
        copies = []
        for d in ORDER:
            copy = remote(
                quarter.at[x, k], quarter.at[x, k], s_q.at[k, d - 1], r_q.at[k, d - 1], x_peer(d)
            )
            copy.start()
            copies.append(copy)
        sends.extend(copies)
        return copies

    lane = lax.broadcasted_iota(jnp.int32, (2, Q), 1) % 4

    def pick(block, source, f):
        total = jnp.zeros(block.shape, F32)
        for g in range(4):
            moved = block if g == f else pltpu.roll(block, (f - g) % 256, axis=1)
            total = jnp.where(source == g, moved, total)
        return jnp.where(lane == f, total[:, :Q], 0.0)

    def right_sides(sweep):
        for n in range(4):
            picked = jnp.zeros((2, Q), F32)
            for f in range(4):
                entry = nb[n, f]
                picked = picked + pick(hb[sweep][entry // 4], entry % 4, f)
            lhs[2 * n : 2 * n + 2, :] = picked
        whole = lhs[...]
        rows = []
        for row in range(8):
            got = dot3(whole, fo[row // 2, row % 2])
            rows.append(res[row : row + 1, :] - got[row : row + 1, :])
        return rows

    def send_local(sweep, rows):
        tails, heads = [], []
        for n in range(4):
            tails.append(rows[2 * n + 1] - apply(element(lo, n, 1), rows[2 * n]))
        for n in range(4):
            heads.append(apply2(element(di, n, 0), rows[2 * n], wb[n, :B, :B], -tails[n]))
            a_out[sweep, n, 0:1, :B] = tails[n]
            a_out[sweep, n, 1:2, :B] = heads[n]
        copies = []
        for d in ORDER:
            copy = remote(
                a_out.at[sweep, (y + d) % 4], a_in.at[sweep, y],
                s_a.at[sweep, d - 1], r_a.at[sweep, d - 1], y_peer(d),
            )
            copy.start()
            copies.append(copy)
        sends.extend(copies)
        a_in[sweep, y] = a_out[sweep, y]
        return copies, tails, heads

    def quarter_tail(sweep):
        tail = [a_in[sweep, j, 0:1, :B] for j in range(4)]
        y2 = tail[1] + apply(seg(0, 1), tail[0])
        y3 = tail[2] + apply(seg(0, 2), y2)
        return (None, tail[0], y2, y3), tail[3] + apply(seg(0, 3), y3)

    def send_quarter_vectors(sweep, starts, tail):
        head = [a_in[sweep, j, 1:2, :B] for j in range(4)]
        g3 = head[3] + apply(seg(2, 3), starts[3])
        g2 = head[2] + apply2(seg(2, 2), starts[2], seg(1, 2), g3)
        g1 = head[1] + apply2(seg(2, 1), starts[1], seg(1, 1), g2)
        th[sweep, x, 0:1, :B] = tail
        th[sweep, x, 1:2, :B] = head[0] + apply(seg(1, 0), g1)
        copies = []
        for d in ORDER:
            copy = remote(
                th.at[sweep, x], th.at[sweep, x], s_x.at[sweep, d - 1], r_x.at[sweep, d - 1], x_peer(d)
            )
            copy.start()
            copies.append(copy)
        sends.extend(copies)
        return copies, (g1, g2, g3)

    def mine(values):
        total = values[0]
        for at in range(1, 4):
            total = jnp.where(x == at, values[at], total)
        return total

    def send_entries(sweep, starts, ends):
        def q(at, k):
            return quarter[at, k, :B, :B]

        tail = [th[sweep, at, 0:1, :B] for at in range(4)]
        head = [th[sweep, at, 1:2, :B] for at in range(4)]
        zero = jnp.zeros((1, B), F32)
        y2 = tail[1] + apply(q(1, 0), tail[0])
        y3 = tail[2] + apply(q(2, 0), y2)
        h3 = head[3] + apply(q(3, 2), y3)
        h2 = head[2] + apply2(q(2, 2), y2, q(2, 1), h3)
        h1 = head[1] + apply2(q(1, 2), tail[0], q(1, 1), h2)
        y_in = mine((zero, tail[0], y2, y3))
        x_in = mine((h1, h2, h3, zero))
        en_out[sweep, 0, 0:1, :B] = y_in
        en_out[sweep, 1, 0:1, :B] = starts[1] + apply(seg(0, 0), y_in)
        en_out[sweep, 2, 0:1, :B] = starts[2] + apply(part[0, :B, :B], y_in)
        en_out[sweep, 3, 0:1, :B] = starts[3] + apply(part[1, :B, :B], y_in)
        en_out[sweep, 0, 1:2, :B] = ends[0] + apply2(
            part[4, :B, :B], y_in, part[6, :B, :B], x_in
        )
        en_out[sweep, 1, 1:2, :B] = ends[1] + apply2(
            part[3, :B, :B], y_in, part[5, :B, :B], x_in
        )
        en_out[sweep, 2, 1:2, :B] = ends[2] + apply2(part[2, :B, :B], y_in, seg(1, 3), x_in)
        en_out[sweep, 3, 1:2, :B] = x_in
        copies = []
        for d in ORDER:
            copy = remote(
                en_out.at[sweep, (y + d) % 4], en_in.at[sweep, y],
                s_e.at[sweep, d - 1], r_e.at[sweep, d - 1], y_peer(d),
            )
            copy.start()
            copies.append(copy)
        sends.extend(copies)
        en_in[sweep, y] = en_out[sweep, y]
        return copies

    def arrived(copies):
        for copy in copies:
            copy.wait_recv()

    def fields(sweep, tails, heads, store):
        for n in range(4):
            y_in = en_in[sweep, n, 0:1, :B]
            x_in = en_in[sweep, n, 1:2, :B]
            tail = tails[n] + apply(own(0, n), y_in)
            store(2 * n, heads[n] + apply2(own(2, n), y_in, own(1, n), x_in))
            store(2 * n + 1, apply2(element(di, n, 1), tail, eb[1, n, :B, :B], -x_in))

    local[0].wait()
    for n in range(4):
        seg_out[0, n, :B, :B] = dot3(element(lo, n, 1), element(lo, n, 0))
    local[1].wait()
    local[2].wait()
    halos = send_halo(0, prev[...])
    maps0 = send_maps(0)
    local[3].wait()
    local[4].wait()
    for n in range(4):
        for l in range(2):
            eb[l, n, :B, :B] = dot3(element(di, n, l), element(up, n, l))
        seg_out[1, n, :B, :B] = dot3(eb[0, n, :B, :B], eb[1, n, :B, :B])
    maps1 = send_maps(1)
    for n in range(4):
        wb[n, :B, :B] = dot3(eb[0, n, :B, :B], element(di, n, 1))
        both = dot3(element(di, n, 0), element(lo, n, 0)) + dot3(wb[n, :B, :B], own(0, n))
        seg_out[2, n, :B, :B] = -both
    maps2 = send_maps(2)
    for k in (5, 6, 7):
        local[k].wait()
    arrived(halos)
    rows = right_sides(0)
    first, tails, heads = send_local(0, rows)
    arrived(maps0)
    p01 = dot3(seg(0, 1), seg(0, 0))
    p23 = dot3(seg(0, 3), seg(0, 2))
    part[0, :B, :B] = p01
    quarters = send_quarter(0, dot3(p23, p01))
    arrived(maps1)
    n01 = dot3(seg(1, 0), seg(1, 1))
    n23 = dot3(seg(1, 2), seg(1, 3))
    part[5, :B, :B] = n23
    quarters += send_quarter(1, dot3(n01, n23))
    arrived(maps2)
    k01 = seg(2, 0) + dot3(seg(1, 0), dot3(seg(2, 1), seg(0, 0)))
    k23 = seg(2, 2) + dot3(seg(1, 2), dot3(seg(2, 3), seg(0, 2)))
    quarters += send_quarter(2, k01 + dot3(n01, dot3(k23, p01)))
    arrived(first)
    starts, tail = quarter_tail(0)
    across, ends = send_quarter_vectors(0, starts, tail)
    p3 = dot3(seg(0, 2), p01)
    part[1, :B, :B] = p3
    k2 = dot3(seg(2, 3), p3)
    part[2, :B, :B] = k2
    k1 = dot3(seg(2, 2), p01) + dot3(seg(1, 2), k2)
    part[3, :B, :B] = k1
    part[4, :B, :B] = dot3(seg(2, 1), seg(0, 0)) + dot3(seg(1, 1), k1)
    part[6, :B, :B] = dot3(seg(1, 1), n23)
    arrived(quarters)
    arrived(across)
    back = send_entries(0, starts, ends)
    arrived(back)

    def keep(row, value):
        f8[row : row + 1, :] = value

    fields(0, tails, heads, keep)
    halos = send_halo(1, f8[...])
    arrived(halos)
    rows = right_sides(1)
    first, tails, heads = send_local(1, rows)
    arrived(first)
    starts, tail = quarter_tail(1)
    across, ends = send_quarter_vectors(1, starts, tail)
    arrived(across)
    back = send_entries(1, starts, ends)
    arrived(back)

    def give(row, value):
        out[row : row + 1, :] = value

    fields(1, tails, heads, give)
    for copy in sends:
        copy.wait_send()


def per_device(residual, previous, lower, pivot, upper, couple, restrict, neighbours):
    def factor(a):
        return jnp.transpose(a, (0, 2, 1, 3)).reshape(4, 2 * B, B)

    dma = pltpu.SemaphoreType.DMA
    result = pl.pallas_call(
        kernel,
        out_shape=jax.ShapeDtypeStruct((8, B), F32),
        in_specs=[pl.BlockSpec(memory_space=pl.ANY)] * 8,
        out_specs=pl.BlockSpec(memory_space=pltpu.VMEM),
        scratch_shapes=[
            pltpu.SMEM((4, 4), jnp.int32),
            pltpu.VMEM((8, B), F32),
            pltpu.VMEM((8, B), F32),
            pltpu.VMEM((Q, B), F32),
            pltpu.VMEM((4, 2 * B, B), F32),
            pltpu.VMEM((4, 2 * B, B), F32),
            pltpu.VMEM((4, 2 * B, B), F32),
            pltpu.VMEM((4, 2, Q, B), F32),
            pltpu.VMEM((2, 4, 104, 128), F32),
            pltpu.VMEM((4, 104, 128), F32),
            pltpu.VMEM((3, 4, 104, 128), F32),
            pltpu.VMEM((3, 4, 104, 128), F32),
            pltpu.VMEM((4, 3, 104, 128), F32),
            pltpu.VMEM((7, 104, 128), F32),
            pltpu.VMEM((12, 2, 256), F32),
            pltpu.VMEM((12, 2, 256), F32),
            pltpu.VMEM((8, Q), F32),
            pltpu.VMEM((8, B), F32),
            pltpu.VMEM((2, 4, 2, 128), F32),
            pltpu.VMEM((2, 4, 2, 128), F32),
            pltpu.VMEM((2, 4, 2, 128), F32),
            pltpu.VMEM((2, 4, 2, 128), F32),
            pltpu.VMEM((2, 4, 2, 128), F32),
            dma((8,)),
            dma((3, 3)),
            dma((3, 3)),
            dma((3, 3)),
            dma((3, 3)),
            dma((2, 2)),
            dma((2, 2)),
            dma((2, 3)),
            dma((2, 3)),
            dma((2, 3)),
            dma((2, 3)),
            dma((2, 3)),
            dma((2, 3)),
        ],
        compiler_params=pltpu.CompilerParams(
            collective_id=0, has_side_effects=True, vmem_limit_bytes=60 << 20
        ),
    )(
        neighbours,
        residual.reshape(8, B),
        previous.reshape(8, B),
        jnp.transpose(restrict, (1, 0, 2)).reshape(Q, B),
        factor(lower),
        factor(pivot),
        factor(upper),
        jnp.transpose(couple, (0, 1, 4, 2, 3)).reshape(4, 2, Q, B),
    )
    return result.reshape(4, 2, B)


def solution(mesh):
    placed = (
        P("patch", "line", None),
        P("patch", "line", None),
        P("patch", "line", None, None),
        P("patch", "line", None, None),
        P("patch", "line", None, None),
        P("patch", "line", None, None, None),
        P(),
        P("patch", None),
    )
    return jax.shard_map(
        per_device, mesh=mesh, in_specs=placed, out_specs=P("patch", "line", None), check_vma=False
    )
```

time: 282 us -> 47.2 us (0.17)
  matrix products: 105 us -> 0 us
  blocking collectives: 88.6 us -> 0 us
  waiting for transfers between devices: 50.6 us -> 0 us
  Pallas kernels: 0 us -> 45.7 us
  between operations: 13.7 us -> 0.01 us
  starting transfers between devices: 12.5 us -> 0 us
  local copies, waits for them, and re-layouts: 5.88 us -> 1.28 us
    dot_general x96 -> x0, matrix products: 105 us -> none  [the longest x86 97.5 us: apply_block(): return jnp.einsum('nab,nb->na', block, vector, precision=HIGH)]
    all_gather x4 -> x0, blocking collectives: 88.6 us -> none  [prefix(): everything = jax.tree.map(lambda part: lax.all_gather(part, axis), shard)]
    all_gather x2 -> x0, waiting for transfers between devices: 46.2 us -> none  [prefix(): everything = jax.tree.map(lambda part: lax.all_gather(part, axis), shard)]
    pallas_call x0 -> x1, Pallas kernels: none -> 45.7 us  [per_device(): pl.pallas_call(kernel, out_shape=jax.ShapeDtypeStruct((8, B), F32), in_sp...]
    ppermute x4 -> x0, starting transfers between devices: 12.4 us -> none  [the longest x2 12.4 us: with_halo(): lax.ppermute(head, axis, [((i + 1) % count, i) for i in range(count)])]
    ppermute x4 -> x0, waiting for transfers between devices: 4.37 us -> none  [the longest x2 2.93 us: with_halo(): lax.ppermute(tail, axis, [(i, (i + 1) % count) for i in range(count)])]
    slice x2 -> x0, local copies, waits for them, and re-layouts: 3.67 us -> none  [the longest x1 2.11 us: backward_pass(): previous = apply_block(pivot_inverse[:, index], inner)]
  transfers between devices with their start and end apart: 6 -> 0, of which waited for: 4 -> 0; matrix products, arithmetic and copies ran while one was open for 12% -> 0% of each run, Pallas kernels for 0% -> 0%
where the time goes in v2:
time: 47.2 us; the launch traced here: 47 us
  Pallas kernels  45.7 us (97%)
  local copies, waits for them, and re-layouts  1.28 us (3%)
    pallas_call x1, Pallas kernels, per_device(): pl.pallas_call(kernel, out_shape=jax.ShapeDtypeStruct((8, B), F32), in_sp...  45.7 us
    unnamed x1, local copies, waits for them, and re-layouts  1.28 us

profile of v2, /device:TPU:6, one launch (start us, length us, event | category | flops | bytes accessed | tf_op | source)
XLA Modules:
  0.0 47.0 jit_solution(14622810477298476202)
XLA Ops:
  0.0 45.7 %shard_map.82 = f32[8,100]{1,0:T(8,128)} custom-call(s32[4,4]{1,0:T(4,128)} %nb_any.1, f32[8,100]{1,0:T(8,128)} %bitcast.24, f32[8,100]{1,0:T(8,128)} %bitcast.25, f32[200,100]{1,0:T(8,128)} %bitcast.22, f32[4,200,100]{2,1,0:T(8,128)} %bitcast.19, f32[4,200,100]{2,1,0:T(8,128)} %bitcast.20, f32[4,200,100]{2,1,0:T(8,128)} %bitcast.21, f32[4,2,200,100]{3,2,1,0:T(8,128)} %bitcast.18), custom_call_target="tpu_custom_call" | custom-call | tf_op jit(solution)/shard_map/pallas_call | solution.py:346
  45.7 1.3 %copy.10 = f32[4,2,100]{2,1,0:T(2,128)} copy(f32[4,2,100]{2,1,0:T(2,128)} %bitcast.23) | data formatting | bytes 6400

commit v3 on v2

v3 whole, which is shorter than its diff:
```python
import jax
import jax.numpy as jnp
from jax import lax
from jax.experimental import pallas as pl
from jax.experimental.pallas import tpu as pltpu
from jax.sharding import PartitionSpec as P

F32 = jnp.float32
BF16 = jnp.bfloat16
MESH = pl.DeviceIdType.MESH
B = 100
Q = 200
NP = 32
NN = (((1,), (0,)), ((), ()))
NT = (((1,), (1,)), ((), ()))


def split(a):
    high = a.astype(BF16)
    return high, (a - high.astype(F32)).astype(BF16)


def dot3(a, b, dims=NN):
    ah, al = split(a)
    bh, bl = split(b)

    def mm(u, v):
        return lax.dot_general(u, v, dims, preferred_element_type=F32)

    return mm(ah, bh) + (mm(ah, bl) + mm(al, bh))


def kernel(
    nb_any, res_any, prev_any, rst_any, low, piv, upp, fc, out,
    nb, res, prev, rst, lo, di, up, fo,
    eb, wb, seg_out, seg_in, quarter, part, hb_first, hb_second, lhs, f16, tr,
    a_out, a_in, th, fx, ob,
    s_loc, s_m, r_m, s_q, r_q, s_h, r_h, s_a, r_a, s_x, r_x, s_t, r_t, s_f, r_f,
):
    p = lax.axis_index("patch")
    line = lax.axis_index("line")
    x, y = line // 4, line % 4
    z, core = p // 2, p % 2
    ys = [(y + d) % 4 for d in range(4)]
    odd = core == 1

    def at(c, d, dz=0):
        return (((z + dz + NP // 2) % (NP // 2)) * 2 + c, x * 4 + ys[d])

    def x_peer(d):
        return (p, ((x + d) % 4) * 4 + y)

    def z_peer(d):
        return ((p + d + NP) % NP, line)

    def remote(src, dst, send, recv, device):
        return pltpu.make_async_remote_copy(
            src_ref=src, dst_ref=dst, send_sem=send, recv_sem=recv,
            device_id=device, device_id_type=MESH,
        )

    barrier = pltpu.get_barrier_semaphore()

    def greet(device):
        pl.semaphore_signal(barrier, inc=1, device_id=device, device_id_type=MESH)

    @pl.when(odd)
    def _():
        for d in (2, 1, 3):
            greet(at(1, d))
            greet(x_peer(d))
        greet(at(0, 0, 1))
        for d in (2, 1, 3, 0):
            greet(at(0, d))

    @pl.when(jnp.logical_not(odd))
    def _():
        for d in (2, 1, 3, 0):
            greet(at(1, d))
        greet(at(1, 0, -1))

    pairs = (
        (low, lo), (prev_any, prev), (rst_any, rst), (piv, di), (upp, up),
        (nb_any, nb), (res_any, res), (fc, fo),
    )
    local = [
        pltpu.make_async_copy(src, dst, s_loc.at[k]) for k, (src, dst) in enumerate(pairs)
    ]
    for copy in local:
        copy.start()

    hb = (hb_first, hb_second)
    sends = []
    sends_even = []
    sends_odd = []
    eye = lax.broadcasted_iota(jnp.int32, (B, B), 0) == lax.broadcasted_iota(
        jnp.int32, (B, B), 1
    )

    def to_row(column):
        return jnp.sum(jnp.where(eye, column, 0.0), axis=0, keepdims=True)

    def apply(matrix, row):
        return to_row(jnp.sum(matrix * row, axis=1, keepdims=True))

    def apply2(one, u, two, v):
        return to_row(jnp.sum(one * u + two * v, axis=1, keepdims=True))

    def element(ref, n, l):
        return ref[n, pl.ds(l, B, stride=2), :]

    def own(k, n):
        return seg_out[k, n, :B, :B]

    def to_owner(src, dst, send, recv):
        def make(d):
            return remote(src(ys[d]), dst(core, y), send.at[d], recv(core, d), at(1, d))

        for d in (2, 1, 3):
            make(d).start()
            sends.append(lambda d=d: make(d))

        @pl.when(jnp.logical_not(odd))
        def _():
            make(0).start()

        sends_even.append(lambda: make(0))

        @pl.when(odd)
        def _():
            dst(1, y)[...] = src(y)[...]

        def wait(d, c):
            remote(src(0), dst(c, 0), send.at[d], recv(c, d), at(1, 1)).wait_recv()

        def arrived():
            for d in (0, 1, 3, 2):
                wait(d, 0)
            for d in (1, 3, 2):
                wait(d, 1)

        return arrived

    def send_maps(k):
        return to_owner(
            lambda n: seg_out.at[k, n], lambda c, j: seg_in.at[c, k, j], s_m.at[k],
            lambda c, d: r_m.at[c, k, d],
        )

    lane = lax.broadcasted_iota(jnp.int32, (2, Q), 1) % 4

    def pick(block, source, f):
        total = jnp.zeros(block.shape, F32)
        for g in range(4):
            moved = block if g == f else pltpu.roll(block, (f - g) % 256, axis=1)
            total = jnp.where(source == g, moved, total)
        return jnp.where(lane == f, total[:, :Q], 0.0)

    def right_sides(sweep):
        for n in range(4):
            picked = jnp.zeros((2, Q), F32)
            for f in range(4):
                entry = nb[n, f]
                picked = picked + pick(
                    hb[sweep][(entry % 16) // 4, entry // 16], entry % 4, f
                )
            lhs[2 * n : 2 * n + 2, :] = picked
        whole = lhs[...]
        rows = []
        for row in range(8):
            got = dot3(whole, fo[row // 2, row % 2])
            rows.append(res[row : row + 1, :] - got[row : row + 1, :])
        return rows

    def send_local(sweep, rows):
        tails = []
        for n in range(4):
            tails.append(rows[2 * n + 1] - apply(element(lo, n, 1), rows[2 * n]))
        for n in range(4):
            a_out[sweep, n, 0:1, :B] = tails[n]
            a_out[sweep, n, 1:2, :B] = apply2(
                element(di, n, 0), rows[2 * n], wb[n, :B, :B], -tails[n]
            )
        return to_owner(
            lambda n: a_out.at[sweep, n], lambda c, j: a_in.at[sweep, c, j], s_a.at[sweep],
            lambda c, d: r_a.at[sweep, c, d],
        )

    both = (0, 1)

    def seg(c, k, j):
        return seg_in[c, k, j, :B, :B]

    def q(c, j, k):
        return quarter[j, k, c, :B, :B]

    def across(make):
        for d in (2, 1, 3):
            make(d).start()
            sends_odd.append(lambda d=d: make(d))

        def arrived():
            for d in (1, 3, 2):
                make(d).wait_recv()

        return arrived

    def send_quarter(k, values):
        for c in both:
            quarter[x, k, c, :B, :B] = values[c]
        return across(
            lambda d: remote(
                quarter.at[x, k], quarter.at[x, k], s_q.at[k, d], r_q.at[k, d], x_peer(d)
            )
        )

    def quarter_tails(sweep):
        tails = [[a_in[sweep, c, j, 0:1, :B] for j in range(4)] for c in both]
        y2 = [tails[c][1] + apply(seg(c, 0, 1), tails[c][0]) for c in both]
        y3 = [tails[c][2] + apply(seg(c, 0, 2), y2[c]) for c in both]
        last = [tails[c][3] + apply(seg(c, 0, 3), y3[c]) for c in both]
        return [(None, tails[c][0], y2[c], y3[c], last[c]) for c in both]

    def send_quarter_vectors(sweep, starts):
        heads = [[a_in[sweep, c, j, 1:2, :B] for j in range(4)] for c in both]
        ends = [[None, None, None, h[3]] for h in heads]
        g3 = [heads[c][3] + apply(seg(c, 2, 3), starts[c][3]) for c in both]
        g2 = [
            heads[c][2] + apply2(seg(c, 2, 2), starts[c][2], seg(c, 1, 2), g3[c]) for c in both
        ]
        g1 = [
            heads[c][1] + apply2(seg(c, 2, 1), starts[c][1], seg(c, 1, 1), g2[c]) for c in both
        ]
        g0 = [heads[c][0] + apply(seg(c, 1, 0), g1[c]) for c in both]
        for c in both:
            th[sweep, x, c, 0:1, :B] = starts[c][4]
            th[sweep, x, c, 1:2, :B] = g0[c]
        arrived = across(
            lambda d: remote(
                th.at[sweep, x], th.at[sweep, x], s_x.at[sweep, d], r_x.at[sweep, d], x_peer(d)
            )
        )
        return arrived, [(g0[c], g1[c], g2[c], g3[c]) for c in both]

    def mine(values):
        total = values[0]
        for j in range(1, 4):
            total = jnp.where(x == j, values[j], total)
        return total

    def fields(sweep, starts, ends):
        tail = [[th[sweep, j, c, 0:1, :B] for j in range(4)] for c in both]
        head = [[th[sweep, j, c, 1:2, :B] for j in range(4)] for c in both]
        zero = jnp.zeros((1, B), F32)
        y2 = [tail[c][1] + apply(q(c, 1, 0), tail[c][0]) for c in both]
        y3 = [tail[c][2] + apply(q(c, 2, 0), y2[c]) for c in both]
        h3 = [head[c][3] + apply(q(c, 3, 2), y3[c]) for c in both]
        h2 = [head[c][2] + apply2(q(c, 2, 2), y2[c], q(c, 2, 1), h3[c]) for c in both]
        h1 = [head[c][1] + apply2(q(c, 1, 2), tail[c][0], q(c, 1, 1), h2[c]) for c in both]
        result = []
        for c in both:
            y_in = mine((zero, tail[c][0], y2[c], y3[c]))
            x_in = mine((h1[c], h2[c], h3[c], zero))
            ahead = [
                starts[c][1] + apply(seg(c, 0, 0), y_in),
                starts[c][2] + apply(part[c, 0, :B, :B], y_in),
                starts[c][3] + apply(part[c, 1, :B, :B], y_in),
                starts[c][4] + apply(quarter[x, 0, c, :B, :B], y_in),
            ]
            g0, g1, g2, g3 = ends[c]
            first = [
                g0 + apply2(quarter[x, 2, c, :B, :B], y_in, quarter[x, 1, c, :B, :B], x_in),
                g1 + apply2(part[c, 4, :B, :B], y_in, part[c, 6, :B, :B], x_in),
                g2 + apply2(part[c, 3, :B, :B], y_in, part[c, 5, :B, :B], x_in),
                g3 + apply2(part[c, 2, :B, :B], y_in, seg(c, 1, 3), x_in),
            ]
            behind = first[1:] + [x_in]
            second = [
                apply2(seg(c, 3, j), ahead[j], seg(c, 4, j), -behind[j]) for j in range(4)
            ]
            result.append((first, second))
        return result

    local[0].wait()
    for n in range(4):
        seg_out[0, n, :B, :B] = dot3(element(lo, n, 1), element(lo, n, 0))
    local[1].wait()
    local[2].wait()
    halo = dot3(prev[...], rst[...], NT)
    for n in range(4):
        hb_first[n, 1, :, :Q] = halo[2 * n : 2 * n + 2]

    @pl.when(odd)
    def _():
        pl.semaphore_wait(barrier, 11)

    @pl.when(jnp.logical_not(odd))
    def _():
        pl.semaphore_wait(barrier, 5)

    halos = []
    for i, dp in enumerate((1, -1)):
        copy = remote(
            hb_first.at[:, 1], hb_first.at[:, 1 - dp], s_h.at[i], r_h.at[i], z_peer(dp)
        )
        copy.start()
        halos.append(copy)
        sends.append(lambda copy=copy: copy)
    maps0 = send_maps(0)
    local[3].wait()
    local[4].wait()
    for n in range(4):
        eb[n, :B, :B] = dot3(element(di, n, 0), element(up, n, 0))
        seg_out[4, n, :B, :B] = dot3(element(di, n, 1), element(up, n, 1))
        seg_out[1, n, :B, :B] = dot3(eb[n, :B, :B], own(4, n))
    maps1 = send_maps(1)
    for n in range(4):
        wb[n, :B, :B] = dot3(eb[n, :B, :B], element(di, n, 1))
        whole = dot3(element(di, n, 0), element(lo, n, 0)) + dot3(wb[n, :B, :B], own(0, n))
        seg_out[2, n, :B, :B] = -whole
    maps2 = send_maps(2)
    for n in range(4):
        seg_out[3, n, :B, :B] = element(di, n, 1)
    maps3 = send_maps(3)
    maps4 = send_maps(4)
    for k in (5, 6, 7):
        local[k].wait()
    for copy in halos:
        copy.wait_recv()
    first_in = send_local(0, right_sides(0))

    def send_traces(j, d):
        same = remote(
            tr.at[j], hb_second.at[y, pl.ds(1, 2)], s_t.at[0, d], r_t.at[0, d], at(0, d)
        )
        beside = remote(
            tr.at[j], hb_second.at[y, pl.ds(0, 2)], s_t.at[1, d], r_t.at[0, d], at(1, d)
        )
        below = remote(
            tr.at[j, 0], hb_second.at[y, 2], s_t.at[2, d], r_t.at[1, d], at(1, d, -1)
        )
        above = remote(
            tr.at[j, 1], hb_second.at[y, 0], s_t.at[3, d], r_t.at[1, d], at(0, d, 1)
        )
        return above, below, same, beside

    @pl.when(odd)
    def _():
        maps0()
        p01 = [dot3(seg(c, 0, 1), seg(c, 0, 0)) for c in both]
        p23 = [dot3(seg(c, 0, 3), seg(c, 0, 2)) for c in both]
        for c in both:
            part[c, 0, :B, :B] = p01[c]
        quarters0 = send_quarter(0, [dot3(p23[c], p01[c]) for c in both])
        maps1()
        n01 = [dot3(seg(c, 1, 0), seg(c, 1, 1)) for c in both]
        n23 = [dot3(seg(c, 1, 2), seg(c, 1, 3)) for c in both]
        for c in both:
            part[c, 5, :B, :B] = n23[c]
        quarters1 = send_quarter(1, [dot3(n01[c], n23[c]) for c in both])
        maps2()
        k1m0 = [dot3(seg(c, 2, 1), seg(c, 0, 0)) for c in both]
        k01 = [seg(c, 2, 0) + dot3(seg(c, 1, 0), k1m0[c]) for c in both]
        k23 = [
            seg(c, 2, 2) + dot3(seg(c, 1, 2), dot3(seg(c, 2, 3), seg(c, 0, 2))) for c in both
        ]
        quarters2 = send_quarter(
            2, [k01[c] + dot3(n01[c], dot3(k23[c], p01[c])) for c in both]
        )
        first_in()
        starts = quarter_tails(0)
        vectors, ends = send_quarter_vectors(0, starts)
        for c in both:
            p3 = dot3(seg(c, 0, 2), p01[c])
            part[c, 1, :B, :B] = p3
            k2 = dot3(seg(c, 2, 3), p3)
            part[c, 2, :B, :B] = k2
            k1 = dot3(seg(c, 2, 2), p01[c]) + dot3(seg(c, 1, 2), k2)
            part[c, 3, :B, :B] = k1
            part[c, 4, :B, :B] = k1m0[c] + dot3(seg(c, 1, 1), k1)
            part[c, 6, :B, :B] = dot3(seg(c, 1, 1), n23[c])
        maps3()
        maps4()
        quarters0()
        quarters1()
        quarters2()
        vectors()
        done = fields(0, starts, ends)
        for c in both:
            first, second = done[c]
            for j in range(4):
                row = 4 * j + 2 * c
                f16[row : row + 1, :] = first[j]
                f16[row + 1 : row + 2, :] = second[j]
        traces = dot3(f16[...], rst[...], NT)
        for j in range(4):
            for c in both:
                row = 4 * j + 2 * c
                tr[j, c, :, :Q] = traces[row : row + 2]
        for d in (2, 1, 3, 0):
            for copy in send_traces(ys[d], d)[: 4 if d else 3]:
                copy.start()
        hb_second[y, pl.ds(0, 2)] = tr[y]

    for d in range(4):
        send_traces(0, d)[0].wait_recv()

    for d in (1, 2, 3):
        send_traces(0, d)[3].wait_recv()

    @pl.when(jnp.logical_not(odd))
    def _():
        send_traces(0, 0)[3].wait_recv()

    second_in = send_local(1, right_sides(1))

    def send_field(d):
        even = remote(fx.at[ys[d], 0], ob.at[y], s_f.at[0, d], r_f.at[d], at(0, d))
        beside = remote(fx.at[ys[d], 1], ob.at[y], s_f.at[1, d], r_f.at[d], at(1, d))
        return even, beside

    @pl.when(odd)
    def _():
        second_in()
        starts = quarter_tails(1)
        vectors, ends = send_quarter_vectors(1, starts)
        vectors()
        done = fields(1, starts, ends)
        for c in both:
            first, second = done[c]
            for j in range(4):
                fx[j, c, 0:1, :B] = first[j]
                fx[j, c, 1:2, :B] = second[j]
        for d in (2, 1, 3, 0):
            for copy in send_field(d)[: 2 if d else 1]:
                copy.start()
        ob[y] = fx[y, 1]

    for d in (1, 2, 3):
        send_field(d)[0].wait_recv()

    @pl.when(jnp.logical_not(odd))
    def _():
        send_field(0)[0].wait_recv()

    for n in range(4):
        out[2 * n : 2 * n + 2, :] = ob[n, :, :B]
    for make in sends:
        make().wait_send()

    @pl.when(jnp.logical_not(odd))
    def _():
        for make in sends_even:
            make().wait_send()

    @pl.when(odd)
    def _():
        for make in sends_odd:
            make().wait_send()
        for d in range(4):
            for copy in send_traces(0, d)[: 4 if d else 3]:
                copy.wait_send()
            for copy in send_field(d)[: 2 if d else 1]:
                copy.wait_send()


def per_device(residual, previous, lower, pivot, upper, couple, restrict, neighbours):
    def factor(a):
        return jnp.transpose(a, (0, 2, 1, 3)).reshape(4, 2 * B, B)

    dma = pltpu.SemaphoreType.DMA
    result = pl.pallas_call(
        kernel,
        out_shape=jax.ShapeDtypeStruct((8, B), F32),
        in_specs=[pl.BlockSpec(memory_space=pl.ANY)] * 8,
        out_specs=pl.BlockSpec(memory_space=pltpu.VMEM),
        scratch_shapes=[
            pltpu.SMEM((4, 4), jnp.int32),
            pltpu.VMEM((8, B), F32),
            pltpu.VMEM((8, B), F32),
            pltpu.VMEM((Q, B), F32),
            pltpu.VMEM((4, 2 * B, B), F32),
            pltpu.VMEM((4, 2 * B, B), F32),
            pltpu.VMEM((4, 2 * B, B), F32),
            pltpu.VMEM((4, 2, Q, B), F32),
            pltpu.VMEM((4, 104, 128), F32),
            pltpu.VMEM((4, 104, 128), F32),
            pltpu.VMEM((5, 4, 104, 128), F32),
            pltpu.VMEM((2, 5, 4, 104, 128), F32),
            pltpu.VMEM((4, 3, 2, 104, 128), F32),
            pltpu.VMEM((2, 7, 104, 128), F32),
            pltpu.VMEM((4, 3, 2, 256), F32),
            pltpu.VMEM((4, 3, 2, 256), F32),
            pltpu.VMEM((8, Q), F32),
            pltpu.VMEM((16, B), F32),
            pltpu.VMEM((4, 2, 2, 256), F32),
            pltpu.VMEM((2, 4, 2, 128), F32),
            pltpu.VMEM((2, 2, 4, 2, 128), F32),
            pltpu.VMEM((2, 4, 2, 2, 128), F32),
            pltpu.VMEM((4, 2, 2, 128), F32),
            pltpu.VMEM((4, 2, 128), F32),
            dma((8,)),
            dma((5, 4)),
            dma((2, 5, 4)),
            dma((3, 4)),
            dma((3, 4)),
            dma((2,)),
            dma((2,)),
            dma((2, 4)),
            dma((2, 2, 4)),
            dma((2, 4)),
            dma((2, 4)),
            dma((4, 4)),
            dma((2, 4)),
            dma((2, 4)),
            dma((4,)),
        ],
        compiler_params=pltpu.CompilerParams(
            collective_id=0, has_side_effects=True, vmem_limit_bytes=60 << 20
        ),
    )(
        neighbours,
        residual.reshape(8, B),
        previous.reshape(8, B),
        jnp.transpose(restrict, (1, 0, 2)).reshape(Q, B),
        factor(lower),
        factor(pivot),
        factor(upper),
        jnp.transpose(couple, (0, 1, 4, 2, 3)).reshape(4, 2, Q, B),
    )
    return result.reshape(4, 2, B)


def solution(mesh):
    placed = (
        P("patch", "line", None),
        P("patch", "line", None),
        P("patch", "line", None, None),
        P("patch", "line", None, None),
        P("patch", "line", None, None),
        P("patch", "line", None, None, None),
        P(),
        P("patch", None),
    )
    return jax.shard_map(
        per_device, mesh=mesh, in_specs=placed, out_specs=P("patch", "line", None), check_vma=False
    )
```

time: 47.2 us -> 50.2 us (1.064)
  the two profiles are of different devices: /device:TPU:6 before, /device:TPU:1 now
where the time goes in v3:
time: 50.2 us; the launch traced here: 50 us
  Pallas kernels  48.7 us (97%)
  local copies, waits for them, and re-layouts  1.28 us (3%)
    pallas_call x1, Pallas kernels, per_device(): pl.pallas_call(kernel, out_shape=jax.ShapeDtypeStruct((8, B), F32), in_sp...  48.7 us
    unnamed x1, local copies, waits for them, and re-layouts  1.28 us

profile of v3, /device:TPU:1, one launch (start us, length us, event | category | flops | bytes accessed | tf_op | source)
XLA Modules:
  0.0 50.0 jit_solution(8894841946656970547)
XLA Ops:
  0.0 48.7 %shard_map.82 = f32[8,100]{1,0:T(8,128)} custom-call(s32[4,4]{1,0:T(4,128)} %nb_any.1, f32[8,100]{1,0:T(8,128)} %bitcast.24, f32[8,100]{1,0:T(8,128)} %bitcast.25, f32[200,100]{1,0:T(8,128)} %bitcast.22, f32[4,200,100]{2,1,0:T(8,128)} %bitcast.19, f32[4,200,100]{2,1,0:T(8,128)} %bitcast.20, f32[4,200,100]{2,1,0:T(8,128)} %bitcast.21, f32[4,2,200,100]{3,2,1,0:T(8,128)} %bitcast.18), custom_call_target="tpu_custom_call" | custom-call | tf_op jit(solution)/shard_map/pallas_call | solution.py:472
  48.8 1.3 %copy.10 = f32[4,2,100]{2,1,0:T(2,128)} copy(f32[4,2,100]{2,1,0:T(2,128)} %bitcast.23) | data formatting | bytes 6400

commit v4 on v3

--- a/solution.py
+++ b/solution.py
@@ -33,9 +33,9 @@
 def kernel(
     nb_any, res_any, prev_any, rst_any, low, piv, upp, fc, out,
     nb, res, prev, rst, lo, di, up, fo,
-    eb, wb, seg_out, seg_in, quarter, part, hb_first, hb_second, lhs, f16, tr,
+    eb, wb, seg_out, seg_in, quarter, part, de, hb_first, hb_second, lhs, f24, ent_out, ent_in,
     a_out, a_in, th, fx, ob,
-    s_loc, s_m, r_m, s_q, r_q, s_h, r_h, s_a, r_a, s_x, r_x, s_t, r_t, s_f, r_f,
+    s_loc, s_d, r_d, s_m, r_m, s_q, r_q, s_h, r_h, s_a, r_a, s_x, r_x, s_t, r_t, s_f, r_f,
 ):
     p = lax.axis_index("patch")
     line = lax.axis_index("line")
@@ -162,7 +162,7 @@
             for f in range(4):
                 entry = nb[n, f]
                 picked = picked + pick(
-                    hb[sweep][(entry % 16) // 4, entry // 16], entry % 4, f
+                    hb[sweep][entry // 4], entry % 4, f
                 )
             lhs[2 * n : 2 * n + 2, :] = picked
         whole = lhs[...]
@@ -275,10 +275,7 @@
                 g3 + apply2(part[c, 2, :B, :B], y_in, seg(c, 1, 3), x_in),
             ]
             behind = first[1:] + [x_in]
-            second = [
-                apply2(seg(c, 3, j), ahead[j], seg(c, 4, j), -behind[j]) for j in range(4)
-            ]
-            result.append((first, second))
+            result.append((first, ahead, behind))
         return result
 
     local[0].wait()
@@ -288,7 +285,7 @@
     local[2].wait()
     halo = dot3(prev[...], rst[...], NT)
     for n in range(4):
-        hb_first[n, 1, :, :Q] = halo[2 * n : 2 * n + 2]
+        hb_first[4 + n, :, :Q] = halo[2 * n : 2 * n + 2]
 
     @pl.when(odd)
     def _():
@@ -301,7 +298,8 @@
     halos = []
     for i, dp in enumerate((1, -1)):
         copy = remote(
-            hb_first.at[:, 1], hb_first.at[:, 1 - dp], s_h.at[i], r_h.at[i], z_peer(dp)
+            hb_first.at[pl.ds(4, 4)], hb_first.at[pl.ds((1 - dp) * 4, 4)], s_h.at[i], r_h.at[i],
+            z_peer(dp),
         )
         copy.start()
         halos.append(copy)
@@ -321,28 +319,39 @@
     maps2 = send_maps(2)
     for n in range(4):
         seg_out[3, n, :B, :B] = element(di, n, 1)
-    maps3 = send_maps(3)
-    maps4 = send_maps(4)
+    beside = []
+    for i, dp in enumerate((1, -1)):
+        copy = remote(
+            seg_out.at[pl.ds(3, 2)], de.at[1 - dp], s_d.at[i], r_d.at[i], z_peer(dp)
+        )
+        copy.start()
+        beside.append(copy)
+        sends.append(lambda copy=copy: copy)
     for k in (5, 6, 7):
         local[k].wait()
     for copy in halos:
         copy.wait_recv()
     first_in = send_local(0, right_sides(0))
-
-    def send_traces(j, d):
+    def send_entries(j, d):
         same = remote(
-            tr.at[j], hb_second.at[y, pl.ds(1, 2)], s_t.at[0, d], r_t.at[0, d], at(0, d)
+            ent_out.at[j], ent_in.at[y, pl.ds(1, 2)], s_t.at[0, d], r_t.at[0, d], at(0, d)
         )
         beside = remote(
-            tr.at[j], hb_second.at[y, pl.ds(0, 2)], s_t.at[1, d], r_t.at[0, d], at(1, d)
+            ent_out.at[j], ent_in.at[y, pl.ds(0, 2)], s_t.at[1, d], r_t.at[0, d], at(1, d)
         )
         below = remote(
-            tr.at[j, 0], hb_second.at[y, 2], s_t.at[2, d], r_t.at[1, d], at(1, d, -1)
+            ent_out.at[j, 0], ent_in.at[y, 2], s_t.at[2, d], r_t.at[1, d], at(1, d, -1)
         )
         above = remote(
-            tr.at[j, 1], hb_second.at[y, 0], s_t.at[3, d], r_t.at[1, d], at(0, d, 1)
+            ent_out.at[j, 1], ent_in.at[y, 0], s_t.at[3, d], r_t.at[1, d], at(0, d, 1)
         )
         return above, below, same, beside
+
+    def store_entries(ref, done):
+        for c in both:
+            for j in range(4):
+                for row in range(3):
+                    ref[j, c, row : row + 1, :B] = done[c][row][j]
 
     @pl.when(odd)
     def _():
@@ -379,39 +388,42 @@
             part[c, 3, :B, :B] = k1
             part[c, 4, :B, :B] = k1m0[c] + dot3(seg(c, 1, 1), k1)
             part[c, 6, :B, :B] = dot3(seg(c, 1, 1), n23[c])
-        maps3()
-        maps4()
         quarters0()
         quarters1()
         quarters2()
         vectors()
         done = fields(0, starts, ends)
-        for c in both:
-            first, second = done[c]
-            for j in range(4):
-                row = 4 * j + 2 * c
-                f16[row : row + 1, :] = first[j]
-                f16[row + 1 : row + 2, :] = second[j]
-        traces = dot3(f16[...], rst[...], NT)
-        for j in range(4):
-            for c in both:
-                row = 4 * j + 2 * c
-                tr[j, c, :, :Q] = traces[row : row + 2]
+        store_entries(ent_out, done)
         for d in (2, 1, 3, 0):
-            for copy in send_traces(ys[d], d)[: 4 if d else 3]:
+            for copy in send_entries(ys[d], d)[: 4 if d else 3]:
                 copy.start()
-        hb_second[y, pl.ds(0, 2)] = tr[y]
-
+        ent_in[y, pl.ds(0, 2)] = ent_out[y]
+
+    for copy in beside:
+        copy.wait_recv()
     for d in range(4):
-        send_traces(0, d)[0].wait_recv()
+        send_entries(0, d)[0].wait_recv()
 
     for d in (1, 2, 3):
-        send_traces(0, d)[3].wait_recv()
+        send_entries(0, d)[3].wait_recv()
 
     @pl.when(jnp.logical_not(odd))
     def _():
-        send_traces(0, 0)[3].wait_recv()
-
+        send_entries(0, 0)[3].wait_recv()
+
+    for o in range(3):
+        for n in range(4):
+            row = 8 * o + 2 * n
+            entry = ent_in[n, o]
+            if o == 1:
+                pivot, upper = own(3, n), own(4, n)
+            else:
+                pivot, upper = de[o, 0, n, :B, :B], de[o, 1, n, :B, :B]
+            f24[row : row + 1, :] = entry[0:1, :B]
+            f24[row + 1 : row + 2, :] = apply2(pivot, entry[1:2, :B], upper, -entry[2:3, :B])
+    halo = dot3(f24[...], rst[...], NT)
+    for m in range(12):
+        hb_second[m, :, :Q] = halo[2 * m : 2 * m + 2]
     second_in = send_local(1, right_sides(1))
 
     def send_field(d):
@@ -426,11 +438,7 @@
         vectors, ends = send_quarter_vectors(1, starts)
         vectors()
         done = fields(1, starts, ends)
-        for c in both:
-            first, second = done[c]
-            for j in range(4):
-                fx[j, c, 0:1, :B] = first[j]
-                fx[j, c, 1:2, :B] = second[j]
+        store_entries(fx, done)
         for d in (2, 1, 3, 0):
             for copy in send_field(d)[: 2 if d else 1]:
                 copy.start()
@@ -444,7 +452,11 @@
         send_field(0)[0].wait_recv()
 
     for n in range(4):
-        out[2 * n : 2 * n + 2, :] = ob[n, :, :B]
+        entry = ob[n]
+        out[2 * n : 2 * n + 1, :] = entry[0:1, :B]
+        out[2 * n + 1 : 2 * n + 2, :] = apply2(
+            own(3, n), entry[1:2, :B], own(4, n), -entry[2:3, :B]
+        )
     for make in sends:
         make().wait_send()
 
@@ -458,7 +470,7 @@
         for make in sends_odd:
             make().wait_send()
         for d in range(4):
-            for copy in send_traces(0, d)[: 4 if d else 3]:
+            for copy in send_entries(0, d)[: 4 if d else 3]:
                 copy.wait_send()
             for copy in send_field(d)[: 2 if d else 1]:
                 copy.wait_send()
@@ -486,22 +498,26 @@
             pltpu.VMEM((4, 104, 128), F32),
             pltpu.VMEM((4, 104, 128), F32),
             pltpu.VMEM((5, 4, 104, 128), F32),
-            pltpu.VMEM((2, 5, 4, 104, 128), F32),
+            pltpu.VMEM((2, 3, 4, 104, 128), F32),
             pltpu.VMEM((4, 3, 2, 104, 128), F32),
             pltpu.VMEM((2, 7, 104, 128), F32),
-            pltpu.VMEM((4, 3, 2, 256), F32),
-            pltpu.VMEM((4, 3, 2, 256), F32),
+            pltpu.VMEM((3, 2, 4, 104, 128), F32),
+            pltpu.VMEM((12, 2, 256), F32),
+            pltpu.VMEM((12, 2, 256), F32),
             pltpu.VMEM((8, Q), F32),
-            pltpu.VMEM((16, B), F32),
-            pltpu.VMEM((4, 2, 2, 256), F32),
+            pltpu.VMEM((24, B), F32),
+            pltpu.VMEM((4, 2, 4, 128), F32),
+            pltpu.VMEM((4, 3, 4, 128), F32),
             pltpu.VMEM((2, 4, 2, 128), F32),
             pltpu.VMEM((2, 2, 4, 2, 128), F32),
             pltpu.VMEM((2, 4, 2, 2, 128), F32),
-            pltpu.VMEM((4, 2, 2, 128), F32),
-            pltpu.VMEM((4, 2, 128), F32),
+            pltpu.VMEM((4, 2, 4, 128), F32),
+            pltpu.VMEM((4, 4, 128), F32),
             dma((8,)),
-            dma((5, 4)),
-            dma((2, 5, 4)),
+            dma((2,)),
+            dma((2,)),
+            dma((3, 4)),
+            dma((2, 3, 4)),
             dma((3, 4)),
             dma((3, 4)),
             dma((2,)),

time: 50.2 us -> 47.8 us (0.952)
  Pallas kernels: 48.7 us -> 46.4 us
    pallas_call x1, Pallas kernels: 48.7 us -> 46.4 us  [per_device(): pl.pallas_call(kernel, out_shape=jax.ShapeDtypeStruct((8, B), F32), in_sp...]
where the time goes in v4:
time: 47.8 us; the launch traced here: 47.6 us
  Pallas kernels  46.4 us (97%)
  local copies, waits for them, and re-layouts  1.28 us (3%)
    pallas_call x1, Pallas kernels, per_device(): pl.pallas_call(kernel, out_shape=jax.ShapeDtypeStruct((8, B), F32), in_sp...  46.4 us
    unnamed x1, local copies, waits for them, and re-layouts  1.28 us

profile of v4, /device:TPU:1, one launch (start us, length us, event | category | flops | bytes accessed | tf_op | source)
XLA Modules:
  0.0 47.6 jit_solution(3186308423320579116)
XLA Ops:
  0.0 46.4 %shard_map.82 = f32[8,100]{1,0:T(8,128)} custom-call(s32[4,4]{1,0:T(4,128)} %nb_any.1, f32[8,100]{1,0:T(8,128)} %bitcast.24, f32[8,100]{1,0:T(8,128)} %bitcast.25, f32[200,100]{1,0:T(8,128)} %bitcast.22, f32[4,200,100]{2,1,0:T(8,128)} %bitcast.19, f32[4,200,100]{2,1,0:T(8,128)} %bitcast.20, f32[4,200,100]{2,1,0:T(8,128)} %bitcast.21, f32[4,2,200,100]{3,2,1,0:T(8,128)} %bitcast.18), custom_call_target="tpu_custom_call" | custom-call | tf_op jit(solution)/shard_map/pallas_call | solution.py:484
  46.4 1.3 %copy.10 = f32[4,2,100]{2,1,0:T(2,128)} copy(f32[4,2,100]{2,1,0:T(2,128)} %bitcast.23) | data formatting | bytes 6400

commit v5 on v4

--- a/solution.py
+++ b/solution.py
@@ -72,12 +72,6 @@
         greet(at(0, 0, 1))
         for d in (2, 1, 3, 0):
             greet(at(0, d))
-
-    @pl.when(jnp.logical_not(odd))
-    def _():
-        for d in (2, 1, 3, 0):
-            greet(at(1, d))
-        greet(at(1, 0, -1))
 
     pairs = (
         (low, lo), (prev_any, prev), (rst_any, rst), (piv, di), (upp, up),
@@ -289,21 +283,33 @@
 
     @pl.when(odd)
     def _():
-        pl.semaphore_wait(barrier, 11)
+        pl.semaphore_wait(barrier, 6)
 
     @pl.when(jnp.logical_not(odd))
     def _():
         pl.semaphore_wait(barrier, 5)
 
-    halos = []
-    for i, dp in enumerate((1, -1)):
-        copy = remote(
+    def halo_to(i, dp):
+        return remote(
             hb_first.at[pl.ds(4, 4)], hb_first.at[pl.ds((1 - dp) * 4, 4)], s_h.at[i], r_h.at[i],
             z_peer(dp),
         )
-        copy.start()
-        halos.append(copy)
-        sends.append(lambda copy=copy: copy)
+
+    def maps_to(i, dp):
+        return remote(
+            seg_out.at[pl.ds(3, 2)], de.at[1 - dp], s_d.at[i], r_d.at[i], z_peer(dp)
+        )
+
+    sides = ((0, 1), (1, -1))
+    for side in sides:
+        sends.append(lambda side=side: halo_to(*side))
+        sends.append(lambda side=side: maps_to(*side))
+
+    @pl.when(jnp.logical_not(odd))
+    def _():
+        for side in sides:
+            halo_to(*side).start()
+
     maps0 = send_maps(0)
     local[3].wait()
     local[4].wait()
@@ -319,18 +325,24 @@
     maps2 = send_maps(2)
     for n in range(4):
         seg_out[3, n, :B, :B] = element(di, n, 1)
-    beside = []
-    for i, dp in enumerate((1, -1)):
-        copy = remote(
-            seg_out.at[pl.ds(3, 2)], de.at[1 - dp], s_d.at[i], r_d.at[i], z_peer(dp)
-        )
-        copy.start()
-        beside.append(copy)
-        sends.append(lambda copy=copy: copy)
     for k in (5, 6, 7):
         local[k].wait()
-    for copy in halos:
-        copy.wait_recv()
+
+    @pl.when(odd)
+    def _():
+        for side, other in zip(sides, sides[::-1]):
+            halo_to(*side).wait_recv()
+            halo_to(*other).start()
+        for side in sides:
+            maps_to(*side).start()
+
+    @pl.when(jnp.logical_not(odd))
+    def _():
+        for side in sides:
+            maps_to(*side).start()
+        for side in sides:
+            halo_to(*side).wait_recv()
+
     first_in = send_local(0, right_sides(0))
     def send_entries(j, d):
         same = remote(
@@ -399,8 +411,8 @@
                 copy.start()
         ent_in[y, pl.ds(0, 2)] = ent_out[y]
 
-    for copy in beside:
-        copy.wait_recv()
+    for side in sides:
+        maps_to(*side).wait_recv()
     for d in range(4):
         send_entries(0, d)[0].wait_recv()
 

time: 47.8 us -> 47.7 us (level)
  no operation moved by 1% of the time
where the time goes in v5:
time: 47.7 us; the launch traced here: 47.5 us
  Pallas kernels  46.2 us (97%)
  local copies, waits for them, and re-layouts  1.28 us (3%)
    pallas_call x1, Pallas kernels, per_device(): pl.pallas_call(kernel, out_shape=jax.ShapeDtypeStruct((8, B), F32), in_sp...  46.2 us
    unnamed x1, local copies, waits for them, and re-layouts  1.28 us

profile of v5, /device:TPU:1, one launch (start us, length us, event | category | flops | bytes accessed | tf_op | source)
XLA Modules:
  0.0 47.5 jit_solution(2617371670676868490)
XLA Ops:
  0.0 46.2 %shard_map.82 = f32[8,100]{1,0:T(8,128)} custom-call(s32[4,4]{1,0:T(4,128)} %nb_any.1, f32[8,100]{1,0:T(8,128)} %bitcast.24, f32[8,100]{1,0:T(8,128)} %bitcast.25, f32[200,100]{1,0:T(8,128)} %bitcast.22, f32[4,200,100]{2,1,0:T(8,128)} %bitcast.19, f32[4,200,100]{2,1,0:T(8,128)} %bitcast.20, f32[4,200,100]{2,1,0:T(8,128)} %bitcast.21, f32[4,2,200,100]{3,2,1,0:T(8,128)} %bitcast.18), custom_call_target="tpu_custom_call" | custom-call | tf_op jit(solution)/shard_map/pallas_call | solution.py:496
  46.2 1.3 %copy.10 = f32[4,2,100]{2,1,0:T(2,128)} copy(f32[4,2,100]{2,1,0:T(2,128)} %bitcast.23) | data formatting | bytes 6400

commit v6 on v5

--- a/solution.py
+++ b/solution.py
@@ -32,7 +32,7 @@
 
 def kernel(
     nb_any, res_any, prev_any, rst_any, low, piv, upp, fc, out,
-    nb, res, prev, rst, lo, di, up, fo,
+    nb, res, prev, rst, lo, di, up, fo, wfc,
     eb, wb, seg_out, seg_in, quarter, part, de, hb_first, hb_second, lhs, f24, ent_out, ent_in,
     a_out, a_in, th, fx, ob,
     s_loc, s_d, r_d, s_m, r_m, s_q, r_q, s_h, r_h, s_a, r_a, s_x, r_x, s_t, r_t, s_f, r_f,
@@ -158,12 +158,15 @@
                 picked = picked + pick(
                     hb[sweep][entry // 4], entry % 4, f
                 )
-            lhs[2 * n : 2 * n + 2, :] = picked
+            lhs[2 * n : 2 * n + 2, :Q] = picked
         whole = lhs[...]
+        high = whole.astype(BF16).astype(F32)
+        halves = jnp.concatenate([high, whole - high], axis=0).astype(BF16)
         rows = []
         for row in range(8):
-            got = dot3(whole, fo[row // 2, row % 2])
-            rows.append(res[row : row + 1, :] - got[row : row + 1, :])
+            got = lax.dot_general(halves, wfc[row], NN, preferred_element_type=F32)
+            low = got[row : row + 1, 128 : 128 + B] + got[row + 8 : row + 9, :B]
+            rows.append(res[row : row + 1, :] - (got[row : row + 1, :B] + low))
         return rows
 
     def send_local(sweep, rows):
@@ -325,8 +328,6 @@
     maps2 = send_maps(2)
     for n in range(4):
         seg_out[3, n, :B, :B] = element(di, n, 1)
-    for k in (5, 6, 7):
-        local[k].wait()
 
     @pl.when(odd)
     def _():
@@ -340,6 +341,19 @@
     def _():
         for side in sides:
             maps_to(*side).start()
+
+    for k in (5, 6, 7):
+        local[k].wait()
+    lhs[:, Q:] = jnp.zeros((8, 8), F32)
+    for row in range(8):
+        high, rest = split(
+            jnp.concatenate([fo[row // 2, row % 2], jnp.zeros((8, B), F32)], axis=0)
+        )
+        wfc[row, :, :B] = high
+        wfc[row, :, 128 : 128 + B] = rest
+
+    @pl.when(jnp.logical_not(odd))
+    def _():
         for side in sides:
             halo_to(*side).wait_recv()
 
@@ -507,6 +521,7 @@
             pltpu.VMEM((4, 2 * B, B), F32),
             pltpu.VMEM((4, 2 * B, B), F32),
             pltpu.VMEM((4, 2, Q, B), F32),
+            pltpu.VMEM((8, Q + 8, 256), BF16),
             pltpu.VMEM((4, 104, 128), F32),
             pltpu.VMEM((4, 104, 128), F32),
             pltpu.VMEM((5, 4, 104, 128), F32),
@@ -516,7 +531,7 @@
             pltpu.VMEM((3, 2, 4, 104, 128), F32),
             pltpu.VMEM((12, 2, 256), F32),
             pltpu.VMEM((12, 2, 256), F32),
-            pltpu.VMEM((8, Q), F32),
+            pltpu.VMEM((8, Q + 8), F32),
             pltpu.VMEM((24, B), F32),
             pltpu.VMEM((4, 2, 4, 128), F32),
             pltpu.VMEM((4, 3, 4, 128), F32),

time: 47.7 us -> 47.5 us (level)
  no operation moved by 1% of the time
where the time goes in v6:
time: 47.5 us; the launch traced here: 47.3 us
  Pallas kernels  46.1 us (97%)
  local copies, waits for them, and re-layouts  1.28 us (3%)
    pallas_call x1, Pallas kernels, per_device(): pl.pallas_call(kernel, out_shape=jax.ShapeDtypeStruct((8, B), F32), in_sp...  46.1 us
    unnamed x1, local copies, waits for them, and re-layouts  1.28 us

profile of v6, /device:TPU:1, one launch (start us, length us, event | category | flops | bytes accessed | tf_op | source)
XLA Modules:
  0.0 47.3 jit_solution(6016526321823148942)
XLA Ops:
  0.0 46.1 %shard_map.82 = f32[8,100]{1,0:T(8,128)} custom-call(s32[4,4]{1,0:T(4,128)} %nb_any.1, f32[8,100]{1,0:T(8,128)} %bitcast.24, f32[8,100]{1,0:T(8,128)} %bitcast.25, f32[200,100]{1,0:T(8,128)} %bitcast.22, f32[4,200,100]{2,1,0:T(8,128)} %bitcast.19, f32[4,200,100]{2,1,0:T(8,128)} %bitcast.20, f32[4,200,100]{2,1,0:T(8,128)} %bitcast.21, f32[4,2,200,100]{3,2,1,0:T(8,128)} %bitcast.18), custom_call_target="tpu_custom_call" | custom-call | tf_op jit(solution)/shard_map/pallas_call | solution.py:510
  46.1 1.3 %copy.10 = f32[4,2,100]{2,1,0:T(2,128)} copy(f32[4,2,100]{2,1,0:T(2,128)} %bitcast.23) | data formatting | bytes 6400

commit v7 on v6

--- a/solution.py
+++ b/solution.py
@@ -40,12 +40,10 @@
     p = lax.axis_index("patch")
     line = lax.axis_index("line")
     x, y = line // 4, line % 4
-    z, core = p // 2, p % 2
     ys = [(y + d) % 4 for d in range(4)]
-    odd = core == 1
-
-    def at(c, d, dz=0):
-        return (((z + dz + NP // 2) % (NP // 2)) * 2 + c, x * 4 + ys[d])
+
+    def at(d, dp=0):
+        return ((p + dp + NP) % NP, x * 4 + ys[d])
 
     def x_peer(d):
         return (p, ((x + d) % 4) * 4 + y)
@@ -64,15 +62,11 @@
     def greet(device):
         pl.semaphore_signal(barrier, inc=1, device_id=device, device_id_type=MESH)
 
-    @pl.when(odd)
-    def _():
-        for d in (2, 1, 3):
-            greet(at(1, d))
-            greet(x_peer(d))
-        greet(at(0, 0, 1))
-        for d in (2, 1, 3, 0):
-            greet(at(0, d))
-
+    for d in (2, 1, 3):
+        greet(at(d))
+        greet(x_peer(d))
+    greet(at(0, 1))
+    greet(at(0, -1))
     pairs = (
         (low, lo), (prev_any, prev), (rst_any, rst), (piv, di), (upp, up),
         (nb_any, nb), (res_any, res), (fc, fo),
@@ -85,8 +79,6 @@
 
     hb = (hb_first, hb_second)
     sends = []
-    sends_even = []
-    sends_odd = []
     eye = lax.broadcasted_iota(jnp.int32, (B, B), 0) == lax.broadcasted_iota(
         jnp.int32, (B, B), 1
     )
@@ -108,30 +100,16 @@
 
     def to_owner(src, dst, send, recv):
         def make(d):
-            return remote(src(ys[d]), dst(core, y), send.at[d], recv(core, d), at(1, d))
+            return remote(src(ys[d]), dst(0, y), send.at[d], recv(0, d), at(d))
 
         for d in (2, 1, 3):
             make(d).start()
             sends.append(lambda d=d: make(d))
-
-        @pl.when(jnp.logical_not(odd))
-        def _():
-            make(0).start()
-
-        sends_even.append(lambda: make(0))
-
-        @pl.when(odd)
-        def _():
-            dst(1, y)[...] = src(y)[...]
-
-        def wait(d, c):
-            remote(src(0), dst(c, 0), send.at[d], recv(c, d), at(1, 1)).wait_recv()
+        dst(0, y)[...] = src(y)[...]
 
         def arrived():
-            for d in (0, 1, 3, 2):
-                wait(d, 0)
             for d in (1, 3, 2):
-                wait(d, 1)
+                make(d).wait_recv()
 
         return arrived
 
@@ -183,7 +161,7 @@
             lambda c, d: r_a.at[sweep, c, d],
         )
 
-    both = (0, 1)
+    both = (0,)
 
     def seg(c, k, j):
         return seg_in[c, k, j, :B, :B]
@@ -194,7 +172,7 @@
     def across(make):
         for d in (2, 1, 3):
             make(d).start()
-            sends_odd.append(lambda d=d: make(d))
+            sends.append(lambda d=d: make(d))
 
         def arrived():
             for d in (1, 3, 2):
@@ -284,13 +262,7 @@
     for n in range(4):
         hb_first[4 + n, :, :Q] = halo[2 * n : 2 * n + 2]
 
-    @pl.when(odd)
-    def _():
-        pl.semaphore_wait(barrier, 6)
-
-    @pl.when(jnp.logical_not(odd))
-    def _():
-        pl.semaphore_wait(barrier, 5)
+    pl.semaphore_wait(barrier, 8)
 
     def halo_to(i, dp):
         return remote(
@@ -308,11 +280,8 @@
         sends.append(lambda side=side: halo_to(*side))
         sends.append(lambda side=side: maps_to(*side))
 
-    @pl.when(jnp.logical_not(odd))
-    def _():
-        for side in sides:
-            halo_to(*side).start()
-
+    for side in sides:
+        halo_to(*side).start()
     maps0 = send_maps(0)
     local[3].wait()
     local[4].wait()
@@ -329,19 +298,8 @@
     for n in range(4):
         seg_out[3, n, :B, :B] = element(di, n, 1)
 
-    @pl.when(odd)
-    def _():
-        for side, other in zip(sides, sides[::-1]):
-            halo_to(*side).wait_recv()
-            halo_to(*other).start()
-        for side in sides:
-            maps_to(*side).start()
-
-    @pl.when(jnp.logical_not(odd))
-    def _():
-        for side in sides:
-            maps_to(*side).start()
-
+    for side in sides:
+        maps_to(*side).start()
     for k in (5, 6, 7):
         local[k].wait()
     lhs[:, Q:] = jnp.zeros((8, 8), F32)
@@ -352,26 +310,17 @@
         wfc[row, :, :B] = high
         wfc[row, :, 128 : 128 + B] = rest
 
-    @pl.when(jnp.logical_not(odd))
-    def _():
-        for side in sides:
-            halo_to(*side).wait_recv()
-
+    for side in sides:
+        halo_to(*side).wait_recv()
     first_in = send_local(0, right_sides(0))
     def send_entries(j, d):
-        same = remote(
-            ent_out.at[j], ent_in.at[y, pl.ds(1, 2)], s_t.at[0, d], r_t.at[0, d], at(0, d)
-        )
-        beside = remote(
-            ent_out.at[j], ent_in.at[y, pl.ds(0, 2)], s_t.at[1, d], r_t.at[0, d], at(1, d)
-        )
-        below = remote(
-            ent_out.at[j, 0], ent_in.at[y, 2], s_t.at[2, d], r_t.at[1, d], at(1, d, -1)
-        )
-        above = remote(
-            ent_out.at[j, 1], ent_in.at[y, 0], s_t.at[3, d], r_t.at[1, d], at(0, d, 1)
-        )
-        return above, below, same, beside
+        return [
+            remote(
+                ent_out.at[j, 0], ent_in.at[y, 1 - dp], s_t.at[dp + 1, d], r_t.at[dp + 1, d],
+                at(d, dp),
+            )
+            for dp in ((-1, 1, 0) if d else (-1, 1))
+        ]
 
     def store_entries(ref, done):
         for c in both:
@@ -379,63 +328,55 @@
                 for row in range(3):
                     ref[j, c, row : row + 1, :B] = done[c][row][j]
 
-    @pl.when(odd)
-    def _():
-        maps0()
-        p01 = [dot3(seg(c, 0, 1), seg(c, 0, 0)) for c in both]
-        p23 = [dot3(seg(c, 0, 3), seg(c, 0, 2)) for c in both]
-        for c in both:
-            part[c, 0, :B, :B] = p01[c]
-        quarters0 = send_quarter(0, [dot3(p23[c], p01[c]) for c in both])
-        maps1()
-        n01 = [dot3(seg(c, 1, 0), seg(c, 1, 1)) for c in both]
-        n23 = [dot3(seg(c, 1, 2), seg(c, 1, 3)) for c in both]
-        for c in both:
-            part[c, 5, :B, :B] = n23[c]
-        quarters1 = send_quarter(1, [dot3(n01[c], n23[c]) for c in both])
-        maps2()
-        k1m0 = [dot3(seg(c, 2, 1), seg(c, 0, 0)) for c in both]
-        k01 = [seg(c, 2, 0) + dot3(seg(c, 1, 0), k1m0[c]) for c in both]
-        k23 = [
-            seg(c, 2, 2) + dot3(seg(c, 1, 2), dot3(seg(c, 2, 3), seg(c, 0, 2))) for c in both
-        ]
-        quarters2 = send_quarter(
-            2, [k01[c] + dot3(n01[c], dot3(k23[c], p01[c])) for c in both]
-        )
-        first_in()
-        starts = quarter_tails(0)
-        vectors, ends = send_quarter_vectors(0, starts)
-        for c in both:
-            p3 = dot3(seg(c, 0, 2), p01[c])
-            part[c, 1, :B, :B] = p3
-            k2 = dot3(seg(c, 2, 3), p3)
-            part[c, 2, :B, :B] = k2
-            k1 = dot3(seg(c, 2, 2), p01[c]) + dot3(seg(c, 1, 2), k2)
-            part[c, 3, :B, :B] = k1
-            part[c, 4, :B, :B] = k1m0[c] + dot3(seg(c, 1, 1), k1)
-            part[c, 6, :B, :B] = dot3(seg(c, 1, 1), n23[c])
-        quarters0()
-        quarters1()
-        quarters2()
-        vectors()
-        done = fields(0, starts, ends)
-        store_entries(ent_out, done)
-        for d in (2, 1, 3, 0):
-            for copy in send_entries(ys[d], d)[: 4 if d else 3]:
-                copy.start()
-        ent_in[y, pl.ds(0, 2)] = ent_out[y]
+    maps0()
+    p01 = [dot3(seg(c, 0, 1), seg(c, 0, 0)) for c in both]
+    p23 = [dot3(seg(c, 0, 3), seg(c, 0, 2)) for c in both]
+    for c in both:
+        part[c, 0, :B, :B] = p01[c]
+    quarters0 = send_quarter(0, [dot3(p23[c], p01[c]) for c in both])
+    maps1()
+    n01 = [dot3(seg(c, 1, 0), seg(c, 1, 1)) for c in both]
+    n23 = [dot3(seg(c, 1, 2), seg(c, 1, 3)) for c in both]
+    for c in both:
+        part[c, 5, :B, :B] = n23[c]
+    quarters1 = send_quarter(1, [dot3(n01[c], n23[c]) for c in both])
+    maps2()
+    k1m0 = [dot3(seg(c, 2, 1), seg(c, 0, 0)) for c in both]
+    k01 = [seg(c, 2, 0) + dot3(seg(c, 1, 0), k1m0[c]) for c in both]
+    k23 = [
+        seg(c, 2, 2) + dot3(seg(c, 1, 2), dot3(seg(c, 2, 3), seg(c, 0, 2))) for c in both
+    ]
+    quarters2 = send_quarter(
+        2, [k01[c] + dot3(n01[c], dot3(k23[c], p01[c])) for c in both]
+    )
+    first_in()
+    starts = quarter_tails(0)
+    vectors, ends = send_quarter_vectors(0, starts)
+    for c in both:
+        p3 = dot3(seg(c, 0, 2), p01[c])
+        part[c, 1, :B, :B] = p3
+        k2 = dot3(seg(c, 2, 3), p3)
+        part[c, 2, :B, :B] = k2
+        k1 = dot3(seg(c, 2, 2), p01[c]) + dot3(seg(c, 1, 2), k2)
+        part[c, 3, :B, :B] = k1
+        part[c, 4, :B, :B] = k1m0[c] + dot3(seg(c, 1, 1), k1)
+        part[c, 6, :B, :B] = dot3(seg(c, 1, 1), n23[c])
+    quarters0()
+    quarters1()
+    quarters2()
+    vectors()
+    done = fields(0, starts, ends)
+    store_entries(ent_out, done)
+    for d in (2, 1, 3, 0):
+        for copy in send_entries(ys[d], d):
+            copy.start()
+    ent_in[y, 1] = ent_out[y, 0]
 
     for side in sides:
         maps_to(*side).wait_recv()
-    for d in range(4):
-        send_entries(0, d)[0].wait_recv()
-
-    for d in (1, 2, 3):
-        send_entries(0, d)[3].wait_recv()
-
-    @pl.when(jnp.logical_not(odd))
-    def _():
-        send_entries(0, 0)[3].wait_recv()
+    for d in (0, 1, 3, 2):
+        for copy in send_entries(0, d):
+            copy.wait_recv()
 
     for o in range(3):
         for n in range(4):
@@ -453,29 +394,20 @@
     second_in = send_local(1, right_sides(1))
 
     def send_field(d):
-        even = remote(fx.at[ys[d], 0], ob.at[y], s_f.at[0, d], r_f.at[d], at(0, d))
-        beside = remote(fx.at[ys[d], 1], ob.at[y], s_f.at[1, d], r_f.at[d], at(1, d))
-        return even, beside
-
-    @pl.when(odd)
-    def _():
-        second_in()
-        starts = quarter_tails(1)
-        vectors, ends = send_quarter_vectors(1, starts)
-        vectors()
-        done = fields(1, starts, ends)
-        store_entries(fx, done)
-        for d in (2, 1, 3, 0):
-            for copy in send_field(d)[: 2 if d else 1]:
-                copy.start()
-        ob[y] = fx[y, 1]
-
-    for d in (1, 2, 3):
-        send_field(d)[0].wait_recv()
-
-    @pl.when(jnp.logical_not(odd))
-    def _():
-        send_field(0)[0].wait_recv()
+        return remote(fx.at[ys[d], 0], ob.at[y], s_f.at[d], r_f.at[d], at(d))
+
+    second_in()
+    starts = quarter_tails(1)
+    vectors, ends = send_quarter_vectors(1, starts)
+    vectors()
+    done = fields(1, starts, ends)
+    store_entries(fx, done)
+    for d in (2, 1, 3):
+        send_field(d).start()
+    ob[y] = fx[y, 0]
+
+    for d in (1, 3, 2):
+        send_field(d).wait_recv()
 
     for n in range(4):
         entry = ob[n]
@@ -486,20 +418,11 @@
     for make in sends:
         make().wait_send()
 
-    @pl.when(jnp.logical_not(odd))
-    def _():
-        for make in sends_even:
-            make().wait_send()
-
-    @pl.when(odd)
-    def _():
-        for make in sends_odd:
-            make().wait_send()
-        for d in range(4):
-            for copy in send_entries(0, d)[: 4 if d else 3]:
-                copy.wait_send()
-            for copy in send_field(d)[: 2 if d else 1]:
-                copy.wait_send()
+    for d in range(4):
+        for copy in send_entries(0, d):
+            copy.wait_send()
+        if d:
+            send_field(d).wait_send()
 
 
 def per_device(residual, previous, lower, pivot, upper, couple, restrict, neighbours):
@@ -525,37 +448,37 @@
             pltpu.VMEM((4, 104, 128), F32),
             pltpu.VMEM((4, 104, 128), F32),
             pltpu.VMEM((5, 4, 104, 128), F32),
-            pltpu.VMEM((2, 3, 4, 104, 128), F32),
-            pltpu.VMEM((4, 3, 2, 104, 128), F32),
-            pltpu.VMEM((2, 7, 104, 128), F32),
+            pltpu.VMEM((1, 3, 4, 104, 128), F32),
+            pltpu.VMEM((4, 3, 1, 104, 128), F32),
+            pltpu.VMEM((1, 7, 104, 128), F32),
             pltpu.VMEM((3, 2, 4, 104, 128), F32),
             pltpu.VMEM((12, 2, 256), F32),
             pltpu.VMEM((12, 2, 256), F32),
             pltpu.VMEM((8, Q + 8), F32),
             pltpu.VMEM((24, B), F32),
-            pltpu.VMEM((4, 2, 4, 128), F32),
+            pltpu.VMEM((4, 1, 4, 128), F32),
             pltpu.VMEM((4, 3, 4, 128), F32),
             pltpu.VMEM((2, 4, 2, 128), F32),
-            pltpu.VMEM((2, 2, 4, 2, 128), F32),
-            pltpu.VMEM((2, 4, 2, 2, 128), F32),
-            pltpu.VMEM((4, 2, 4, 128), F32),
+            pltpu.VMEM((2, 1, 4, 2, 128), F32),
+            pltpu.VMEM((2, 4, 1, 2, 128), F32),
+            pltpu.VMEM((4, 1, 4, 128), F32),
             pltpu.VMEM((4, 4, 128), F32),
             dma((8,)),
             dma((2,)),
             dma((2,)),
             dma((3, 4)),
-            dma((2, 3, 4)),
+            dma((1, 3, 4)),
             dma((3, 4)),
             dma((3, 4)),
             dma((2,)),
             dma((2,)),
             dma((2, 4)),
-            dma((2, 2, 4)),
+            dma((2, 1, 4)),
             dma((2, 4)),
             dma((2, 4)),
-            dma((4, 4)),
-            dma((2, 4)),
-            dma((2, 4)),
+            dma((3, 4)),
+            dma((3, 4)),
+            dma((4,)),
             dma((4,)),
         ],
         compiler_params=pltpu.CompilerParams(

time: 47.5 us -> 46.2 us (0.973)
  the two profiles are of different devices: /device:TPU:1 before, /device:TPU:6 now
where the time goes in v7:
time: 46.2 us; the launch traced here: 45.9 us
  Pallas kernels  44.7 us (97%)
  local copies, waits for them, and re-layouts  1.28 us (3%)
    pallas_call x1, Pallas kernels, per_device(): pl.pallas_call(kernel, out_shape=jax.ShapeDtypeStruct((8, B), F32), in_sp...  44.7 us
    unnamed x1, local copies, waits for them, and re-layouts  1.28 us

profile of v7, /device:TPU:6, one launch (start us, length us, event | category | flops | bytes accessed | tf_op | source)
XLA Modules:
  0.0 45.9 jit_solution(891798448227260956)
XLA Ops:
  0.0 44.7 %shard_map.82 = f32[8,100]{1,0:T(8,128)} custom-call(s32[4,4]{1,0:T(4,128)} %nb_any.1, f32[8,100]{1,0:T(8,128)} %bitcast.24, f32[8,100]{1,0:T(8,128)} %bitcast.25, f32[200,100]{1,0:T(8,128)} %bitcast.22, f32[4,200,100]{2,1,0:T(8,128)} %bitcast.19, f32[4,200,100]{2,1,0:T(8,128)} %bitcast.20, f32[4,200,100]{2,1,0:T(8,128)} %bitcast.21, f32[4,2,200,100]{3,2,1,0:T(8,128)} %bitcast.18), custom_call_target="tpu_custom_call" | custom-call | tf_op jit(solution)/shard_map/pallas_call | solution.py:433
  44.7 1.3 %copy.10 = f32[4,2,100]{2,1,0:T(2,128)} copy(f32[4,2,100]{2,1,0:T(2,128)} %bitcast.23) | data formatting | bytes 6400

commit v8 on v7

--- a/solution.py
+++ b/solution.py
@@ -298,8 +298,6 @@
     for n in range(4):
         seg_out[3, n, :B, :B] = element(di, n, 1)
 
-    for side in sides:
-        maps_to(*side).start()
     for k in (5, 6, 7):
         local[k].wait()
     lhs[:, Q:] = jnp.zeros((8, 8), F32)
@@ -313,13 +311,14 @@
     for side in sides:
         halo_to(*side).wait_recv()
     first_in = send_local(0, right_sides(0))
-    def send_entries(j, d):
+    def send_entries(j, d, steps=(-1, 1, 0)):
         return [
             remote(
                 ent_out.at[j, 0], ent_in.at[y, 1 - dp], s_t.at[dp + 1, d], r_t.at[dp + 1, d],
                 at(d, dp),
             )
-            for dp in ((-1, 1, 0) if d else (-1, 1))
+            for dp in steps
+            if d or dp
         ]
 
     def store_entries(ref, done):
@@ -340,27 +339,33 @@
     for c in both:
         part[c, 5, :B, :B] = n23[c]
     quarters1 = send_quarter(1, [dot3(n01[c], n23[c]) for c in both])
+    for side in sides:
+        maps_to(*side).start()
+    p3 = [dot3(seg(c, 0, 2), p01[c]) for c in both]
+    n02 = [dot3(n01[c], seg(c, 1, 2)) for c in both]
+    for c in both:
+        part[c, 1, :B, :B] = p3[c]
+        part[c, 6, :B, :B] = dot3(seg(c, 1, 1), n23[c])
     maps2()
     k1m0 = [dot3(seg(c, 2, 1), seg(c, 0, 0)) for c in both]
-    k01 = [seg(c, 2, 0) + dot3(seg(c, 1, 0), k1m0[c]) for c in both]
-    k23 = [
-        seg(c, 2, 2) + dot3(seg(c, 1, 2), dot3(seg(c, 2, 3), seg(c, 0, 2))) for c in both
-    ]
+    k2m1 = [dot3(seg(c, 2, 2), p01[c]) for c in both]
+    k3m2 = [dot3(seg(c, 2, 3), p3[c]) for c in both]
     quarters2 = send_quarter(
-        2, [k01[c] + dot3(n01[c], dot3(k23[c], p01[c])) for c in both]
+        2,
+        [
+            (seg(c, 2, 0) + dot3(seg(c, 1, 0), k1m0[c]))
+            + (dot3(n01[c], k2m1[c]) + dot3(n02[c], k3m2[c]))
+            for c in both
+        ],
     )
     first_in()
     starts = quarter_tails(0)
     vectors, ends = send_quarter_vectors(0, starts)
     for c in both:
-        p3 = dot3(seg(c, 0, 2), p01[c])
-        part[c, 1, :B, :B] = p3
-        k2 = dot3(seg(c, 2, 3), p3)
-        part[c, 2, :B, :B] = k2
-        k1 = dot3(seg(c, 2, 2), p01[c]) + dot3(seg(c, 1, 2), k2)
+        part[c, 2, :B, :B] = k3m2[c]
+        k1 = k2m1[c] + dot3(seg(c, 1, 2), k3m2[c])
         part[c, 3, :B, :B] = k1
         part[c, 4, :B, :B] = k1m0[c] + dot3(seg(c, 1, 1), k1)
-        part[c, 6, :B, :B] = dot3(seg(c, 1, 1), n23[c])
     quarters0()
     quarters1()
     quarters2()
@@ -372,13 +377,7 @@
             copy.start()
     ent_in[y, 1] = ent_out[y, 0]
 
-    for side in sides:
-        maps_to(*side).wait_recv()
-    for d in (0, 1, 3, 2):
-        for copy in send_entries(0, d):
-            copy.wait_recv()
-
-    for o in range(3):
+    def second_elements(o):
         for n in range(4):
             row = 8 * o + 2 * n
             entry = ent_in[n, o]
@@ -388,6 +387,17 @@
                 pivot, upper = de[o, 0, n, :B, :B], de[o, 1, n, :B, :B]
             f24[row : row + 1, :] = entry[0:1, :B]
             f24[row + 1 : row + 2, :] = apply2(pivot, entry[1:2, :B], upper, -entry[2:3, :B])
+
+    for side in sides:
+        maps_to(*side).wait_recv()
+    for d in (1, 3, 2):
+        send_entries(0, d, (0,))[0].wait_recv()
+    second_elements(1)
+    for d in (0, 1, 3, 2):
+        for copy in send_entries(0, d, (-1, 1)):
+            copy.wait_recv()
+    second_elements(0)
+    second_elements(2)
     halo = dot3(f24[...], rst[...], NT)
     for m in range(12):
         hb_second[m, :, :Q] = halo[2 * m : 2 * m + 2]

time: 46.2 us -> 46.1 us (level)
  Pallas kernels: 44.7 us -> 44.2 us
    pallas_call x1, Pallas kernels: 44.7 us -> 44.2 us  [per_device(): pl.pallas_call(kernel, out_shape=jax.ShapeDtypeStruct((8, B), F32), in_sp...]
where the time goes in v8:
time: 46.1 us; the launch traced here: 45.5 us
  Pallas kernels  44.2 us (96%)
  local copies, waits for them, and re-layouts  1.28 us (3%)
    pallas_call x1, Pallas kernels, per_device(): pl.pallas_call(kernel, out_shape=jax.ShapeDtypeStruct((8, B), F32), in_sp...  44.2 us
    unnamed x1, local copies, waits for them, and re-layouts  1.28 us

profile of v8, /device:TPU:6, one launch (start us, length us, event | category | flops | bytes accessed | tf_op | source)
XLA Modules:
  0.0 45.5 jit_solution(15483397061897623562)
XLA Ops:
  0.0 44.2 %shard_map.82 = f32[8,100]{1,0:T(8,128)} custom-call(s32[4,4]{1,0:T(4,128)} %nb_any.1, f32[8,100]{1,0:T(8,128)} %bitcast.24, f32[8,100]{1,0:T(8,128)} %bitcast.25, f32[200,100]{1,0:T(8,128)} %bitcast.22, f32[4,200,100]{2,1,0:T(8,128)} %bitcast.19, f32[4,200,100]{2,1,0:T(8,128)} %bitcast.20, f32[4,200,100]{2,1,0:T(8,128)} %bitcast.21, f32[4,2,200,100]{3,2,1,0:T(8,128)} %bitcast.18), custom_call_target="tpu_custom_call" | custom-call | tf_op jit(solution)/shard_map/pallas_call | solution.py:443
  44.2 1.3 %copy.10 = f32[4,2,100]{2,1,0:T(2,128)} copy(f32[4,2,100]{2,1,0:T(2,128)} %bitcast.23) | data formatting | bytes 6400

commit v9 on v8

--- a/solution.py
+++ b/solution.py
@@ -298,6 +298,8 @@
     for n in range(4):
         seg_out[3, n, :B, :B] = element(di, n, 1)
 
+    for side in sides:
+        maps_to(*side).start()
     for k in (5, 6, 7):
         local[k].wait()
     lhs[:, Q:] = jnp.zeros((8, 8), F32)
@@ -339,8 +341,6 @@
     for c in both:
         part[c, 5, :B, :B] = n23[c]
     quarters1 = send_quarter(1, [dot3(n01[c], n23[c]) for c in both])
-    for side in sides:
-        maps_to(*side).start()
     p3 = [dot3(seg(c, 0, 2), p01[c]) for c in both]
     n02 = [dot3(n01[c], seg(c, 1, 2)) for c in both]
     for c in both:

time: 46.1 us -> 46.1 us (level)
  no operation moved by 1% of the time
where the time goes in v9:
time: 46.1 us; the launch traced here: 45.5 us
  Pallas kernels  44.2 us (96%)
  local copies, waits for them, and re-layouts  1.28 us (3%)
    pallas_call x1, Pallas kernels, per_device(): pl.pallas_call(kernel, out_shape=jax.ShapeDtypeStruct((8, B), F32), in_sp...  44.2 us
    unnamed x1, local copies, waits for them, and re-layouts  1.28 us

profile of v9, /device:TPU:6, one launch (start us, length us, event | category | flops | bytes accessed | tf_op | source)
XLA Modules:
  0.0 45.5 jit_solution(2201865559499700415)
XLA Ops:
  0.0 44.2 %shard_map.82 = f32[8,100]{1,0:T(8,128)} custom-call(s32[4,4]{1,0:T(4,128)} %nb_any.1, f32[8,100]{1,0:T(8,128)} %bitcast.24, f32[8,100]{1,0:T(8,128)} %bitcast.25, f32[200,100]{1,0:T(8,128)} %bitcast.22, f32[4,200,100]{2,1,0:T(8,128)} %bitcast.19, f32[4,200,100]{2,1,0:T(8,128)} %bitcast.20, f32[4,200,100]{2,1,0:T(8,128)} %bitcast.21, f32[4,2,200,100]{3,2,1,0:T(8,128)} %bitcast.18), custom_call_target="tpu_custom_call" | custom-call | tf_op jit(solution)/shard_map/pallas_call | solution.py:443
  44.2 1.3 %copy.10 = f32[4,2,100]{2,1,0:T(2,128)} copy(f32[4,2,100]{2,1,0:T(2,128)} %bitcast.23) | data formatting | bytes 6400
